TPU v7x, 32 devices: a whole 2x2x4 slice. The times are simulated.
32 devices in a mesh: dp: 8 (over z, x), tensor: 4 (over y, core).
Axes of the slice: x: 2, y: 2, z: 4, core: 2. Of those that a mesh axis runs over, the one named last changes fastest.
Arguments:
- tokens: bfloat16 [16384, 768], P(('dp', 'tensor')), may hold values from -6 to 6
- ln1_gain: float32 [768], replicated, may hold values from 0.5 to 1.5
- ln1_shift: float32 [768], replicated, may hold values from -2 to 2
- qkv_weight: bfloat16 [3, 768, 768], P(None, None, 'tensor'), may hold values from -0.21875 to 0.21875
- qv_bias: float32 [2, 768], P(None, 'tensor'), may hold values from -2 to 2
- out_weight: bfloat16 [768, 768], P('tensor'), may hold values from -1.75 to 1.75
- out_bias: float32 [768], replicated, may hold values from -2 to 2
- ln2_gain: float32 [768], replicated, may hold values from 0.5 to 1.5
- ln2_shift: float32 [768], replicated, may hold values from -2 to 2
- fc_weight: bfloat16 [768, 3072], P(None, 'tensor'), may hold values from -0.21875 to 0.21875
- fc_bias: float32 [3072], P('tensor'), may hold values from -2 to 2
- proj_weight: bfloat16 [3072, 768], P('tensor'), may hold values from -0.109375 to 0.109375
- proj_bias: float32 [768], replicated, may hold values from -2 to 2
- cotangent: bfloat16 [16384, 768], P(('dp', 'tensor')), may hold values from -6 to 6
Outputs:
- output: bfloat16 [16384, 768], P(('dp', 'tensor'))
- tokens_grad: float32 [16384, 768], P(('dp', 'tensor'))
- ln1_gain_grad: float32 [768], replicated
- ln1_shift_grad: float32 [768], replicated
- qkv_weight_grad: float32 [3, 768, 768], P(None, None, 'tensor')
- qv_bias_grad: float32 [2, 768], P(None, 'tensor')
- out_weight_grad: float32 [768, 768], P('tensor')
- out_bias_grad: float32 [768], replicated
- ln2_gain_grad: float32 [768], replicated
- ln2_shift_grad: float32 [768], replicated
- fc_weight_grad: float32 [768, 3072], P(None, 'tensor')
- fc_bias_grad: float32 [3072], P('tensor')
- proj_weight_grad: float32 [3072, 768], P('tensor')
- proj_bias_grad: float32 [768], replicated
All inputs are finite; a program needn't handle non-finite values.
Results may differ from a plain program's by a relative error of at most 0.018.
Values may be sent and summed in bfloat16 or wider, within the bound.
A program may use at most 128 MiB of HBM per device.

v0:
```python
from functools import partial

import jax
import jax.numpy as jnp
from jax import lax
from jax.sharding import PartitionSpec as P

D = 768
HEAD_DIM = 64
LEN = 1024


NORM_EPSILON = 1e-05


def normalize(values):
    row_mean = jnp.mean(values, axis=-1, keepdims=True)
    centred = values - row_mean
    variance = jnp.mean(centred * centred, axis=-1, keepdims=True)
    row_scale = lax.rsqrt(variance + NORM_EPSILON)
    return (centred * row_scale, row_scale)


def norm_back(grad_in, normed, row_scale, gain_vec):
    shaped = grad_in * gain_vec
    return row_scale * (
        shaped
        - jnp.mean(shaped, axis=-1, keepdims=True)
        - normed * jnp.mean(shaped * normed, axis=-1, keepdims=True)
    )


def causal_scores(query, key_rows):
    length = query.shape[1]
    raw_scores = jnp.einsum(
        "hqd,hkd->hqk", query, key_rows, preferred_element_type=jnp.float32
    ) * HEAD_DIM ** (-0.5)
    causal = lax.broadcasted_iota(jnp.int32, (length, length), 0) >= lax.broadcasted_iota(
        jnp.int32, (length, length), 1
    )
    return jnp.where(causal[None], raw_scores, -1e30)


def attend_forward(seq_block):
    scores = causal_scores(seq_block[0], seq_block[1])
    row_max = jnp.max(scores, axis=-1, keepdims=True)
    exponent = jnp.exp(scores - row_max)
    row_total = jnp.sum(exponent, axis=-1, keepdims=True)
    weights = (exponent / row_total).astype(jnp.bfloat16)
    attended = jnp.einsum("hqk,hkd->hqd", weights, seq_block[2], preferred_element_type=jnp.float32)
    return (attended.astype(jnp.bfloat16), row_max[..., 0] + jnp.log(row_total[..., 0]))


def attend_backward(packed):
    seq_block, log_total, out_grad = packed
    factor = HEAD_DIM ** (-0.5)
    scores = causal_scores(seq_block[0], seq_block[1])
    weights = jnp.exp(scores - log_total[:, :, None])
    value_grad = jnp.einsum(
        "hqk,hqd->hkd", weights.astype(jnp.bfloat16), out_grad, preferred_element_type=jnp.float32
    )
    weight_grad = jnp.einsum(
        "hqd,hkd->hqk", out_grad, seq_block[2], preferred_element_type=jnp.float32
    )
    score_grad = (
        weights * (weight_grad - jnp.sum(weights * weight_grad, axis=-1, keepdims=True))
    ).astype(jnp.bfloat16)
    query_grad = (
        jnp.einsum("hqk,hkd->hqd", score_grad, seq_block[1], preferred_element_type=jnp.float32)
        * factor
    )
    key_grad = (
        jnp.einsum("hqk,hqd->hkd", score_grad, seq_block[0], preferred_element_type=jnp.float32)
        * factor
    )
    return jnp.stack([query_grad, key_grad, value_grad]).astype(jnp.bfloat16)


def local(
    tokens,
    ln1_gain,
    ln1_shift,
    qkv_weight,
    qv_bias,
    out_weight,
    out_bias,
    ln2_gain,
    ln2_shift,
    fc_weight,
    fc_bias,
    proj_weight,
    proj_bias,
    cotangent,
):
    tok_rows = tokens.astype(jnp.float32)
    own_rows = tok_rows.shape[0]
    normed1, scale1 = normalize(tok_rows)
    first_low = (normed1 * ln1_gain + ln1_shift).astype(jnp.bfloat16)
    first_full = lax.all_gather(first_low, "tensor", axis=0, tiled=True)
    width = qkv_weight.shape[2]
    local_heads = width // HEAD_DIM
    qkv_flat = jnp.transpose(qkv_weight, (1, 0, 2)).reshape(D, 3 * width)
    qkv_shift = jnp.concatenate([qv_bias[0], jnp.zeros((width,), jnp.float32), qv_bias[1]])
    qkv_low = (
        jnp.dot(first_full, qkv_flat, preferred_element_type=jnp.float32) + qkv_shift
    ).astype(jnp.bfloat16)
    full_rows = qkv_low.shape[0]
    sequences = full_rows // LEN
    seq_blocks = qkv_low.reshape(sequences, LEN, 3, local_heads, HEAD_DIM).transpose(0, 2, 3, 1, 4)
    attended, log_total = lax.map(attend_forward, seq_blocks)
    heads_flat = attended.transpose(0, 2, 1, 3).reshape(full_rows, width)
    branch_sum = lax.psum_scatter(
        jnp.dot(heads_flat, out_weight, preferred_element_type=jnp.float32).astype(jnp.bfloat16),
        "tensor",
        scatter_dimension=0,
        tiled=True,
    ).astype(jnp.float32)
    resid = tok_rows + branch_sum + out_bias
    normed2, scale2 = normalize(resid)
    second_low = (normed2 * ln2_gain + ln2_shift).astype(jnp.bfloat16)
    second_full = lax.all_gather(second_low, "tensor", axis=0, tiled=True)
    hidden = jnp.dot(second_full, fc_weight, preferred_element_type=jnp.float32) + fc_bias
    active, gelu_back = jax.vjp(partial(jax.nn.gelu, approximate=True), hidden)
    active_low = active.astype(jnp.bfloat16)
    mlp_out = lax.psum_scatter(
        jnp.dot(
            lax.slice_in_dim(active_low, 0, own_rows * lax.axis_size("tensor"), axis=0),
            proj_weight,
            preferred_element_type=jnp.float32,
        ).astype(jnp.bfloat16),
        "tensor",
        scatter_dimension=0,
        tiled=True,
    ).astype(jnp.float32)
    output = (resid + mlp_out + proj_bias).astype(jnp.bfloat16)
    grad_rows = cotangent.astype(jnp.float32)
    proj_bias_grad = jnp.sum(grad_rows, axis=0)
    grad_full = lax.all_gather(cotangent, "tensor", axis=0, tiled=True)
    proj_weight_grad = jnp.einsum(
        "fh,fd->hd", active_low, grad_full, preferred_element_type=jnp.float32
    )
    active_grad = jnp.einsum(
        "fd,hd->fh", grad_full, proj_weight, preferred_element_type=jnp.float32
    )
    hidden_low = gelu_back(active_grad)[0].astype(jnp.bfloat16)
    fc_bias_grad = jnp.sum(hidden_low, axis=0, dtype=jnp.float32)
    fc_weight_grad = jnp.einsum(
        "fd,fh->dh", second_full, hidden_low, preferred_element_type=jnp.float32
    )
    second_grad = lax.psum_scatter(
        jnp.einsum("fh,dh->fd", hidden_low, fc_weight, preferred_element_type=jnp.float32).astype(
            jnp.bfloat16
        ),
        "tensor",
        scatter_dimension=0,
        tiled=True,
    ).astype(jnp.float32)
    resid_grad = grad_rows + norm_back(second_grad, normed2, scale2, ln2_gain)
    branch_low = resid_grad.astype(jnp.bfloat16)
    branch_full = lax.all_gather(branch_low, "tensor", axis=0, tiled=True)
    ln2_gain_grad = jnp.sum(second_grad * normed2, axis=0)
    ln2_shift_grad = jnp.sum(second_grad, axis=0)
    out_bias_grad = jnp.sum(branch_low, axis=0, dtype=jnp.float32)
    out_weight_grad = jnp.einsum(
        "fw,fd->wd", heads_flat, branch_full, preferred_element_type=jnp.float32
    )
    heads_grad = jnp.einsum(
        "fd,wd->fw", branch_full, out_weight, preferred_element_type=jnp.float32
    ).astype(jnp.bfloat16)
    heads_grad = heads_grad.reshape(sequences, LEN, local_heads, HEAD_DIM).transpose(0, 2, 1, 3)
    block_grads = lax.map(attend_backward, (seq_blocks, log_total, heads_grad))
    qkv_grad_low = block_grads.transpose(0, 3, 1, 2, 4).reshape(full_rows, 3 * width)
    column_sums = jnp.sum(qkv_grad_low, axis=0, dtype=jnp.float32).reshape(3, width)
    qv_bias_grad = jnp.stack([column_sums[0], column_sums[2]])
    qkv_weight_grad = jnp.einsum(
        "fd,fc->dc", first_full, qkv_grad_low, preferred_element_type=jnp.float32
    )
    qkv_weight_grad = qkv_weight_grad.reshape(D, 3, width).transpose(1, 0, 2)
    first_grad = lax.psum_scatter(
        jnp.einsum("fc,dc->fd", qkv_grad_low, qkv_flat, preferred_element_type=jnp.float32).astype(
            jnp.bfloat16
        ),
        "tensor",
        scatter_dimension=0,
        tiled=True,
    ).astype(jnp.float32)
    ln1_gain_grad = jnp.sum(first_grad * normed1, axis=0)
    ln1_shift_grad = jnp.sum(first_grad, axis=0)
    tokens_grad = resid_grad + norm_back(first_grad, normed1, scale1, ln1_gain)
    (
        qkv_weight_grad,
        qv_bias_grad,
        out_weight_grad,
        fc_weight_grad,
        fc_bias_grad,
        proj_weight_grad,
    ) = lax.psum(
        (
            qkv_weight_grad,
            qv_bias_grad,
            out_weight_grad,
            fc_weight_grad,
            fc_bias_grad,
            proj_weight_grad,
        ),
        "dp",
    )
    ln1_gain_grad, ln1_shift_grad, out_bias_grad, ln2_gain_grad, ln2_shift_grad, proj_bias_grad = (
        lax.psum(
            (
                ln1_gain_grad,
                ln1_shift_grad,
                out_bias_grad,
                ln2_gain_grad,
                ln2_shift_grad,
                proj_bias_grad,
            ),
            ("dp", "tensor"),
        )
    )
    return (
        output,
        tokens_grad,
        ln1_gain_grad,
        ln1_shift_grad,
        qkv_weight_grad,
        qv_bias_grad,
        out_weight_grad,
        out_bias_grad,
        ln2_gain_grad,
        ln2_shift_grad,
        fc_weight_grad,
        fc_bias_grad,
        proj_weight_grad,
        proj_bias_grad,
    )


def solution(mesh):
    return jax.shard_map(
        local,
        mesh=mesh,
        in_specs=(
            P(("dp", "tensor"), None),
            P(),
            P(),
            P(None, None, "tensor"),
            P(None, "tensor"),
            P("tensor", None),
            P(),
            P(),
            P(),
            P(None, "tensor"),
            P("tensor"),
            P("tensor", None),
            P(),
            P(("dp", "tensor"), None),
        ),
        out_specs=(
            P(("dp", "tensor"), None),
            P(("dp", "tensor"), None),
            P(),
            P(),
            P(None, None, "tensor"),
            P(None, "tensor"),
            P("tensor", None),
            P(),
            P(),
            P(),
            P(None, "tensor"),
            P("tensor"),
            P("tensor", None),
            P(),
        ),
        check_vma=False,
    )
```

profile of v0, /device:TPU:0, one launch (start us, length us, event | category | flops | bytes accessed | tf_op | source)
XLA Modules:
  0.0 726.6 jit_solution(3653023267619387123)
XLA Ops:
  13.3 31.2 %all-gather.5.cloned.1.call-done = bf16[2048,768]{1,0:T(8,128)(2,1)} async-done(((bf16[512,768]{1,0:T(8,128)(2,1)}), bf16[2048,768]{1,0:T(8,128)(2,1)}) %all-gather.5.cloned.1.call-update) | async-done | bytes 3145744 | tf_op jit(solution)/shard_map/all_gather | solution.py:99
  54.0 42.8 %while.22 = (s32[]{:T(128)}, bf16[2,3,1024,64]{2,3,1,0:T(8,128)(2,1)}, f32[2,3,1024]{2,1,0:T(4,128)}, bf16[2,3,3,1024,64]{3,4,2,1,0:T(8,128)(2,1)S(1)}, s32[]{:T(128)}, /*index=5*/s32[]{:T(128)}, s32[]{}, s32[]{}) while((s32[]{:T(128)}, bf16[2,3,1024,64]{2,3,1,0:T(8,128)(2,1)}, f32[2,3,1024]{2,1,0:T(4,128)}, ...), condition=%wide.region_5.6_spmd, body=%wide.region_2.5_spmd.sunk | while | flops 844297216 | bytes 49921200 | solution.py:110
  54.4 5.9 fusion.117
  60.3 7.4 %fusion.118 = f32[3,1024]{1,0:T(4,128)S(1)} fusion(f32[3,1024,1024]{1,2,0:T(8,128)} %get-tuple-element.178, f32[3,1024]{1,0:T(4,128)S(1)} %get-tuple-element.179, pred[1024,1024]{0,1:T(8,128)(4,1)S(1)} %iota_compare_fusion.4), kind=kLoop, calls=%fused_computation.4.clone.1 | loop fusion | flops 12579840 | bytes 13656064 | tf_op jit(solution)/shard_map/while/body/eval_jaxpr/reduce_sum | solution.py:48
  67.7 6.8 fusion.119
  75.8 5.9 fusion.117
  81.7 7.4 %fusion.118 = f32[3,1024]{1,0:T(4,128)S(1)} fusion(f32[3,1024,1024]{1,2,0:T(8,128)} %get-tuple-element.178, f32[3,1024]{1,0:T(4,128)S(1)} %get-tuple-element.179, pred[1024,1024]{0,1:T(8,128)(4,1)S(1)} %iota_compare_fusion.4), kind=kLoop, calls=%fused_computation.4.clone.1 | loop fusion | flops 12579840 | bytes 13656064 | tf_op jit(solution)/shard_map/while/body/eval_jaxpr/reduce_sum | solution.py:48
  89.1 6.8 fusion.119
  103.6 37.8 %reduce-scatter.5.cloned.1.call-done = bf16[512,768]{1,0:T(8,128)(2,1)} async-done(((bf16[2048,768]{1,0:T(8,128)(2,1)}), bf16[512,768]{1,0:T(8,128)(2,1)}) %reduce-scatter.5.cloned.1.call-update) | async-done | bytes 786448 | tf_op jit(solution)/shard_map/reduce_scatter | solution.py:112
  146.5 28.1 %all-gather.7.cloned.1.call-done = bf16[2048,768]{1,0:T(8,128)(2,1)} async-done(((bf16[512,768]{1,0:T(8,128)(2,1)}), bf16[2048,768]{1,0:T(8,128)(2,1)}) %all-gather.7.cloned.1.call-update) | async-done | bytes 3145744 | tf_op jit(solution)/shard_map/all_gather | solution.py:121
  174.6 7.5 %fusion.77 = f32[2048,768]{1,0:T(8,128)} fusion(bf16[2048,768]{1,0:T(8,128)(2,1)} %all-gather.7.cloned.1.call-done, bf16[768,768]{1,0:T(8,128)(2,1)} %param.27), kind=kOutput, calls=%fused_computation.127 | convolution fusion | flops 2415919104 | bytes 10616832 | tf_op jit(solution)/shard_map/dot_general | solution.py:122
  182.1 22.6 %all-gather.9.cloned.1.call-done = bf16[2048,768]{1,0:T(8,128)(2,1)} async-done(((bf16[512,768]{1,0:T(8,128)(2,1)}), bf16[2048,768]{1,0:T(8,128)(2,1)}) %all-gather.9.cloned.1.call-update) | async-done | bytes 3145744 | tf_op jit(solution)/shard_map/all_gather | solution.py:138
  204.6 12.4 %convert_reduce_fusion = (f32[768]{0:T(1024)}, bf16[2048,768]{1,0:T(8,128)(2,1)S(1)}, bf16[2048,768]{1,0:T(8,128)(2,1)}) fusion(f32[2048,768]{1,0:T(8,128)} %fusion.77, f32[768]{0:T(1024)S(1)} %copy-done.42, bf16[2048,768]{1,0:T(8,128)(2,1)} %all-gather.9.cloned.1.call-done, bf16[768,768]{1,0:T(8,128)(2,1)S(1)} %copy-done), kind=kOutput, calls=%fused_computation.61 | convolution fusion | flops 2455239936 | bytes 16914432 | tf_op jit(solution)/shard_map/fd,hd->fh/dot_general | solution.py:142
  222.7 6.2 convolution_convert_fusion.1
  229.0 10.4 %all-gather.11.cloned.1.call-start = ((), (), s32[]{:S(2)}) async-start(), calls=%async_computation.10 | async-start | bytes 3932160 | tf_op jit(solution)/shard_map/all_gather | solution.py:160
  239.4 21.4 %reduce-scatter.9.cloned.1.call-done = bf16[512,768]{1,0:T(8,128)(2,1)} async-done(((bf16[2048,768]{1,0:T(8,128)(2,1)}), bf16[512,768]{1,0:T(8,128)(2,1)}) %reduce-scatter.9.cloned.1.call-update) | async-done | bytes 786448 | tf_op jit(solution)/shard_map/reduce_scatter | solution.py:150
  263.5 37.6 %reduce-scatter.7.cloned.1.call-done = bf16[512,768]{1,0:T(8,128)(2,1)} async-done(((bf16[2048,768]{1,0:T(8,128)(2,1)}), bf16[512,768]{1,0:T(8,128)(2,1)}) %reduce-scatter.7.cloned.1.call-update) | async-done | bytes 786448 | tf_op jit(solution)/shard_map/reduce_scatter | solution.py:125
  301.1 4.6 convert_reduce_fusion.6
  305.8 28.6 %all-gather.11.cloned.1.call-done = bf16[2048,768]{1,0:T(8,128)(2,1)} async-done(((bf16[512,768]{1,0:T(8,128)(2,1)}), bf16[2048,768]{1,0:T(8,128)(2,1)}) %all-gather.11.cloned.1.call-update) | async-done | bytes 3145744 | tf_op jit(solution)/shard_map/all_gather | solution.py:160
  339.2 83.0 %while.23 = (s32[]{:T(128)}, bf16[2,3,3,1024,64]{3,4,2,1,0:T(8,128)(2,1)}, bf16[2,3,3,1024,64]{3,4,2,1,0:T(8,128)(2,1)}, f32[2,3,1024]{2,1,0:T(4,128)}, bf16[2,3...) while((s32[]{:T(128)}, bf16[2,3,3,1024,64]{3,4,2,1,0:T(8,128)(2,1)}, ...), condition=%wide.region_15.16_spmd, body=%wide.region_13.15_spmd.sunk | while | flops 2066019328 | bytes 163142960 | solution.py:171
  340.2 7.5 %fusion.124 = f32[3,1024,1024]{1,2,0:T(8,128)} fusion(bf16[2,3,3,1024,64]{3,4,2,1,0:T(8,128)(2,1)} %get-tuple-element.231, s32[]{:T(128)S(6)} %copy.66, s32[]{:T(128)S(6)} %add.261), kind=kOutput, calls=%fused_computation.43.clone.1 | convolution fusion | flops 402653184 | bytes 13370880 | tf_op jit(solution)/shard_map/while/body/eval_jaxpr/hqd,hkd->hqk/dot_general | solution.py:35
  347.7 8.9 %fusion.125 = bf16[1,1,3,1024,64]{3,4,2,1,0:T(8,128)(2,1)} fusion(f32[3,1024,1024]{1,2,0:T(8,128)} %fusion.124, f32[3,1024]{1,0:T(4,128)S(1)} %dynamic-slice_bitcast_fusion.26, pred[1024,1024]{0,1:T(8,128)(4,1)S(1)} %iota_compare_fusion.5, bf16[2,3,1024,64]{2,3,1,0:T(8,128)(2,1)} %get-tuple-element.233, s32[]{:T(128)S(6)} %copy.66), kind=kOutput, calls=%fused_computation.31.clone.1 | convolution fusion | flops 415432704 | bytes 14430212 | tf_op jit(solution)/shard_map/while/body/eval_jaxpr/hqk,hqd->hkd/dot_general | solution.py:59
  356.6 10.0 %multiply_reduce_fusion.3 = (f32[3,1024]{1,0:T(4,128)S(1)}, f32[3,1024,1024]{1,2,0:T(8,128)}) fusion(f32[3,1024,1024]{1,2,0:T(8,128)} %fusion.124, f32[3,1024]{1,0:T(4,128)S(1)} %dynamic-slice_bitcast_fusion.26, pred[1024,1024]{0,1:T(8,128)(4,1)S(1)} %iota_compare_fusion.5, bf16[2,3,3,1024,64]{3,4,2,1,0:T(8,128)(2,1)} %get-tuple-element.231, ...), kind=kOutput, calls=%fused_computation.20.clone.1 | convolution fusion | flops 418378752 | bytes 27026944 | tf_op jit(solution)/shard_map/while/body/eval_jaxpr/hqd,hkd->hqk/dot_general | solution.py:62
  366.6 7.0 multiply_convert_fusion.3
  381.6 7.5 %fusion.124 = f32[3,1024,1024]{1,2,0:T(8,128)} fusion(bf16[2,3,3,1024,64]{3,4,2,1,0:T(8,128)(2,1)} %get-tuple-element.231, s32[]{:T(128)S(6)} %copy.66, s32[]{:T(128)S(6)} %add.261), kind=kOutput, calls=%fused_computation.43.clone.1 | convolution fusion | flops 402653184 | bytes 13370880 | tf_op jit(solution)/shard_map/while/body/eval_jaxpr/hqd,hkd->hqk/dot_general | solution.py:35
  389.1 8.9 %fusion.125 = bf16[1,1,3,1024,64]{3,4,2,1,0:T(8,128)(2,1)} fusion(f32[3,1024,1024]{1,2,0:T(8,128)} %fusion.124, f32[3,1024]{1,0:T(4,128)S(1)} %dynamic-slice_bitcast_fusion.26, pred[1024,1024]{0,1:T(8,128)(4,1)S(1)} %iota_compare_fusion.5, bf16[2,3,1024,64]{2,3,1,0:T(8,128)(2,1)} %get-tuple-element.233, s32[]{:T(128)S(6)} %copy.66), kind=kOutput, calls=%fused_computation.31.clone.1 | convolution fusion | flops 415432704 | bytes 14430212 | tf_op jit(solution)/shard_map/while/body/eval_jaxpr/hqk,hqd->hkd/dot_general | solution.py:59
  398.0 10.0 %multiply_reduce_fusion.3 = (f32[3,1024]{1,0:T(4,128)S(1)}, f32[3,1024,1024]{1,2,0:T(8,128)}) fusion(f32[3,1024,1024]{1,2,0:T(8,128)} %fusion.124, f32[3,1024]{1,0:T(4,128)S(1)} %dynamic-slice_bitcast_fusion.26, pred[1024,1024]{0,1:T(8,128)(4,1)S(1)} %iota_compare_fusion.5, bf16[2,3,3,1024,64]{3,4,2,1,0:T(8,128)(2,1)} %get-tuple-element.231, ...), kind=kOutput, calls=%fused_computation.20.clone.1 | convolution fusion | flops 418378752 | bytes 27026944 | tf_op jit(solution)/shard_map/while/body/eval_jaxpr/hqd,hkd->hqk/dot_general | solution.py:62
  408.0 7.0 multiply_convert_fusion.3
  431.6 7.1 fusion.80
  451.0 22.0 %all-reduce.1 = (f32[2,192]{1,0:T(2,128)}, f32[768]{0:T(1024)}) all-reduce(f32[2,192]{1,0:T(2,128)S(1)} %pad_maximum_fusion.1, f32[768]{0:T(1024)S(1)} %copy-done.36), channel_id=1, replica_groups=mesh['dp'=8,'tensor'=4] {'dp'}, use_global_device_ids=true, to_apply=%region_25.26 | all-reduce | flops 1152 | bytes 9216 | tf_op jit(solution)/shard_map/psum | solution.py:197
  474.9 40.6 %all-reduce = (f32[768]{0:T(1024)}, f32[768]{0:T(1024)}, f32[768]{0:T(1024)}, f32[768]{0:T(1024)}, f32[768]{0:T(1024)}, /*index=5*/f32[768]{0:T(1024)}) all-reduce(f32[768]{0:T(1024)S(1)} %get-tuple-element.69, f32[768]{0:T(1024)S(1)} %get-tuple-element.74, ...), channel_id=1, replica_groups=mesh['dp'=8,'tensor'=4] {'dp','tensor'}, use_global_device_ids=true, to_apply=%region_20.21 | all-reduce | flops 4608 | bytes 36864 | tf_op jit(solution)/shard_map/psum | solution.py:209
  518.4 193.6 %all-reduce.5.cloned.1.call-done = (f32[3,768,192]{1,2,0:T(8,128)}, f32[192,768]{1,0:T(8,128)}, f32[768,768]{1,0:T(8,128)}, f32[768,768]{1,0:T(8,128)}) async-done(((f32[3,768,192]{1,2,0:T(8,128)}, f32[192,768]{1,0:T(8,128)}, f32[768,768]{1,0:T(8,128)}, f32[768,768]{1,0:T(8,128)}), (f32[3,768,192]{1,2,0:T(8,128)}, f32[192,768]{1,0:T(8,128)}, f32[768,768]{1,0:T(8,128)}, ...) | async-done | bytes 7077904 | tf_op jit(solution)/shard_map/psum | solution.py:197
  (193 shorter events, 93.0 us)
Async XLA Ops:
  7.2 197.4 %copy-start = (bf16[768,768]{1,0:T(8,128)(2,1)S(1)}, bf16[768,768]{1,0:T(8,128)(2,1)}, u32[]{:S(2)}) copy-start(bf16[768,768]{1,0:T(8,128)(2,1)} %param.29) | copy-start | bytes 3538948
  7.2 37.4 %all-gather.5.cloned.1.call-start = ((), (), s32[]{:S(2)}) async-start(), calls=%async_computation.4 | async-start | bytes 3932160 | tf_op jit(solution)/shard_map/all_gather | solution.py:99
  13.2 128.2 %reduce-scatter.5.cloned.1.call-start = ((), (), s32[]{:S(2)}) async-start(), calls=%async_computation.5 | async-start | bytes 3932160 | tf_op jit(solution)/shard_map/reduce_scatter | solution.py:112
  103.2 38.1 %copy-start.2 = (bf16[512,768]{1,0:T(8,128)(2,1)S(1)}, bf16[512,768]{1,0:T(8,128)(2,1)}, u32[]{:S(2)}) copy-start(bf16[512,768]{1,0:T(8,128)(2,1)} %param.18) | copy-start | bytes 2359300
  103.2 38.1 %copy-start.23 = (f32[768]{0:T(1024)S(1)}, f32[768]{0:T(1024)}, u32[]{:S(2)}) copy-start(f32[768]{0:T(1024)} %param.24) | copy-start | bytes 9220
  103.2 41.3 %copy-start.26 = (f32[768]{0:T(1024)S(1)}, f32[768]{0:T(1024)}, u32[]{:S(2)}) copy-start(f32[768]{0:T(1024)} %param.25) | copy-start | bytes 9220
  103.2 41.3 %copy-start.34 = (f32[768]{0:T(1024)S(1)}, f32[768]{0:T(1024)}, u32[]{:S(2)}) copy-start(f32[768]{0:T(1024)} %param.26) | copy-start | bytes 9220
  103.2 71.3 %all-gather.7.cloned.1.call-start = ((), (), s32[]{:S(2)}) async-start(), calls=%async_computation.6 | async-start | bytes 3932160 | tf_op jit(solution)/shard_map/all_gather | solution.py:121
  145.9 58.8 %all-gather.9.cloned.1.call-start = ((), (), s32[]{:S(2)}) async-start(), calls=%async_computation.8 | async-start | bytes 3932160 | tf_op jit(solution)/shard_map/all_gather | solution.py:138
  146.4 58.2 %copy-start.42 = (f32[768]{0:T(1024)S(1)}, f32[768]{0:T(1024)}, u32[]{:S(2)}) copy-start(f32[768]{0:T(1024)} %param.28) | copy-start | bytes 9220
  146.5 114.3 %reduce-scatter.9.cloned.1.call-start = ((), (), s32[]{:S(2)}) async-start(), calls=%async_computation.9 | async-start | bytes 3932160 | tf_op jit(solution)/shard_map/reduce_scatter | solution.py:150
  222.7 78.4 %reduce-scatter.7.cloned.1.call-start = ((), (), s32[]{:S(2)}) async-start(), calls=%async_computation.7 | async-start | bytes 3932160 | tf_op jit(solution)/shard_map/reduce_scatter | solution.py:125
  228.9 72.2 %copy-start.14 = (bf16[512,768]{1,0:T(8,128)(2,1)S(1)}, bf16[512,768]{1,0:T(8,128)(2,1)}, u32[]{:S(2)}) copy-start(bf16[512,768]{1,0:T(8,128)(2,1)} %param.31) | copy-start | bytes 2359300
  228.9 72.2 %copy-start.35 = (f32[768]{0:T(1024)S(1)}, f32[768]{0:T(1024)}, u32[]{:S(2)}) copy-start(f32[768]{0:T(1024)} %param.30) | copy-start | bytes 9220
  229.0 105.5 %all-gather.11.cloned.1.call-start = ((), (), s32[]{:S(2)}) async-start(), calls=%async_computation.10 | async-start | bytes 3932160 | tf_op jit(solution)/shard_map/all_gather | solution.py:160
  260.8 40.4 %copy-start.15 = (bf16[512,768]{1,0:T(8,128)(2,1)S(1)}, bf16[512,768]{1,0:T(8,128)(2,1)}, u32[]{:S(2)}) copy-start(bf16[512,768]{1,0:T(8,128)(2,1)} %reduce-scatter.9.cloned.1.call-done) | copy-start | bytes 2359300
  301.1 33.3 %copy-start.22 = (bf16[192,768]{1,0:T(8,128)(2,1)S(1)}, bf16[192,768]{1,0:T(8,128)(2,1)}, u32[]{:S(2)}) copy-start(bf16[192,768]{1,0:T(8,128)(2,1)} %param.23) | copy-start | bytes 884740
  305.7 167.2 %reduce-scatter.11.cloned.1.call-start = ((), (), s32[]{:S(2)}) async-start(), calls=%async_computation.11 | async-start | bytes 3932160 | tf_op jit(solution)/shard_map/reduce_scatter | solution.py:179
  347.7 18.9 %slice-start = ((s8[12582912]{0:T(1024)(128)(4,1)}), s8[4194304]{0:T(1024)(128)(4,1)S(1)}, s32[]{:S(2)}) async-start(s8[12582912]{0:T(1024)(128)(4,1)} %bitcast.147), calls=%async_computation.13 | async-start | bytes 8388608 | tf_op jit(solution)/shard_map/while
  347.7 18.9 %slice-start.1 = ((s8[12582912]{0:T(1024)(128)(4,1)}), s8[4194304]{0:T(1024)(128)(4,1)S(1)}, s32[]{:S(2)}) async-start(s8[12582912]{0:T(1024)(128)(4,1)} %bitcast.147), calls=%async_computation.14 | async-start | bytes 8388608 | tf_op jit(solution)/shard_map/while
  389.1 18.9 %slice-start = ((s8[12582912]{0:T(1024)(128)(4,1)}), s8[4194304]{0:T(1024)(128)(4,1)S(1)}, s32[]{:S(2)}) async-start(s8[12582912]{0:T(1024)(128)(4,1)} %bitcast.147), calls=%async_computation.13 | async-start | bytes 8388608 | tf_op jit(solution)/shard_map/while
  389.1 18.9 %slice-start.1 = ((s8[12582912]{0:T(1024)(128)(4,1)}), s8[4194304]{0:T(1024)(128)(4,1)S(1)}, s32[]{:S(2)}) async-start(s8[12582912]{0:T(1024)(128)(4,1)} %bitcast.147), calls=%async_computation.14 | async-start | bytes 8388608 | tf_op jit(solution)/shard_map/while
  431.5 280.5 %all-reduce.5.cloned.1.call-start = ((), (), s32[]{:S(2)}) async-start(), calls=%async_computation.12 | async-start | bytes 14155776 | tf_op jit(solution)/shard_map/psum | solution.py:197
  450.3 22.7 %copy-start.3 = (bf16[512,768]{1,0:T(8,128)(2,1)S(1)}, bf16[512,768]{1,0:T(8,128)(2,1)}, u32[]{:S(2)}) copy-start(bf16[512,768]{1,0:T(8,128)(2,1)} %param.18) | copy-start | bytes 2359300
  450.3 22.7 %copy-start.25 = (f32[512]{0:T(512)S(1)}, f32[512]{0:T(512)}, u32[]{:S(2)}) copy-start(f32[512]{0:T(512)} %copy-done.24) | copy-start | bytes 6148
  450.3 22.7 %copy-start.27 = (f32[768]{0:T(1024)S(1)}, f32[768]{0:T(1024)}, u32[]{:S(2)}) copy-start(f32[768]{0:T(1024)} %param.19) | copy-start | bytes 9220
  450.3 22.7 %copy-start.29 = (f32[512]{0:T(512)S(1)}, f32[512]{0:T(512)}, u32[]{:S(2)}) copy-start(f32[512]{0:T(512)} %copy-done.28) | copy-start | bytes 6148
  450.3 24.6 %copy-start.30 = (f32[768]{0:T(1024)S(1)}, f32[768]{0:T(1024)}, u32[]{:S(2)}) copy-start(f32[768]{0:T(1024)} %get-tuple-element.67) | copy-start | bytes 9220
  450.3 24.6 %copy-start.31 = (f32[768]{0:T(1024)S(1)}, f32[768]{0:T(1024)}, u32[]{:S(2)}) copy-start(f32[768]{0:T(1024)} %get-tuple-element.73) | copy-start | bytes 9220
  450.3 24.6 %copy-start.32 = (f32[768]{0:T(1024)S(1)}, f32[768]{0:T(1024)}, u32[]{:S(2)}) copy-start(f32[768]{0:T(1024)} %get-tuple-element.107) | copy-start | bytes 9220
  450.3 24.6 %copy-start.33 = (f32[768]{0:T(1024)S(1)}, f32[768]{0:T(1024)}, u32[]{:S(2)}) copy-start(f32[768]{0:T(1024)} %get-tuple-element.116) | copy-start | bytes 9220
  450.7 64.8 %copy-start.12 = (f32[512,768]{1,0:T(8,128)S(1)}, f32[512,768]{1,0:T(8,128)}, u32[]{:S(2)}) copy-start(f32[512,768]{1,0:T(8,128)} %get-tuple-element.109) | copy-start | bytes 4718596
  (33 other events, 128.3 us)
Sparse Core Ops, SparseCore 0:
  13.3 31.2 all-gather.4
  103.3 37.9 reduce-scatter.4
  146.0 28.5 all-gather.6
  176.0 28.5 all-gather.8
  222.8 37.9 reduce-scatter.8
  263.2 37.9 reduce-scatter.6
  305.9 28.5 all-gather.10
  431.6 37.9 reduce-scatter.10
  475.2 236.7 all-reduce.4
where the time goes:
time: 736 us; the launch traced here: 727 us
  waiting for transfers between devices  401 us (54%)
  matrix products  149 us (20%)
  blocking collectives  62.6 us (9%)
  other arithmetic  53.9 us (7%)
  local copies, waits for them, and re-layouts  33.3 us (5%)
  between operations  14.6 us (2%)
  starting transfers between devices  11 us (1%)
    psum x1, waiting for transfers between devices, local(): lax.psum((qkv_weight_grad, qv_bias_grad, out_weight_grad, fc_weight_grad,...  194 us
    psum x1, blocking collectives, local(): lax.psum((ln1_gain_grad, ln1_shift_grad, out_bias_grad, ln2_gain_grad, ln...  40.6 us
    reduce_scatter x1, waiting for transfers between devices, local(): lax.psum_scatter(jnp.dot(heads_flat, out_weight, preferred_element_type=j...  37.8 us
    reduce_scatter x1, waiting for transfers between devices, local(): lax.psum_scatter(jnp.dot(lax.slice_in_dim(active_low, 0, own_rows * lax.a...  37.6 us
    all_gather x1, waiting for transfers between devices, local(): first_full = lax.all_gather(first_low, 'tensor', axis=0, tiled=True)  31.2 us
    all_gather x1, waiting for transfers between devices, local(): branch_full = lax.all_gather(branch_low, 'tensor', axis=0, tiled=True)  28.6 us
    all_gather x1, waiting for transfers between devices, local(): second_full = lax.all_gather(second_low, 'tensor', axis=0, tiled=True)  28.1 us
    dot_general x4, matrix products, causal_scores(): jnp.einsum('hqd,hkd->hqk', query, key_rows, preferred_element_type=jnp.fl...  26.8 us
  transfers between devices with their start and end apart: 9, of which 8 were waited for; matrix products, arithmetic and copies ran while one was open for 5% of the time, Pallas kernels for 0%

commit v1 on v0

v1 whole, which is shorter than its diff:
```python
from functools import partial

import jax
import jax.numpy as jnp
from jax import lax
from jax.experimental import pallas as pl
from jax.experimental.pallas import tpu as pltpu
from jax.sharding import PartitionSpec as P

HEAD_DIM = 64
PAIR = 2 * HEAD_DIM
LEN = 1024
BLOCK = 256
NORM_EPSILON = 1e-05
SCORE_SCALE = 1.4426950408889634 * HEAD_DIM**-0.5

ROWS_ROWS = (((1,), (1,)), ((), ()))


def normalize(values):
    row_mean = jnp.mean(values, axis=-1, keepdims=True)
    centred = values - row_mean
    variance = jnp.mean(centred * centred, axis=-1, keepdims=True)
    row_scale = lax.rsqrt(variance + NORM_EPSILON)
    return (centred * row_scale, row_scale)


def norm_back(grad_in, normed, row_scale, gain_vec):
    shaped = grad_in * gain_vec
    return row_scale * (
        shaped
        - jnp.mean(shaped, axis=-1, keepdims=True)
        - normed * jnp.mean(shaped * normed, axis=-1, keepdims=True)
    )


def dot32(left, right, dims=(((1,), (0,)), ((), ()))):
    return lax.dot_general(left, right, dims, preferred_element_type=jnp.float32)


def half_starts(core_ref):
    half = LEN // 2
    first = pl.multiple_of(core_ref[0] * half, half)
    second = pl.multiple_of(half - core_ref[0] * half, half)
    return first, second


def in_order(ref, starts):
    half = LEN // 2
    return jnp.concatenate([ref[pl.ds(start, half), :] for start in starts], axis=0)


def block_rows(starts, step):
    half = LEN // 2
    offset = step * BLOCK
    start = starts[offset // half] + offset % half
    return pl.ds(pl.multiple_of(start, BLOCK), BLOCK)


def split_heads(block):
    low_lanes = lax.broadcasted_iota(jnp.int32, block.shape, 1) < HEAD_DIM
    zero = jnp.zeros_like(block)
    return jnp.concatenate(
        [jnp.where(low_lanes, block, zero), jnp.where(low_lanes, zero, block)], axis=0
    )


def causal_keep():
    keys = lax.broadcasted_iota(jnp.int32, (BLOCK, 2 * BLOCK), 0)
    queries = lax.broadcasted_iota(jnp.int32, (BLOCK, 2 * BLOCK), 1) % BLOCK
    return keys <= queries


def attend_forward_kernel(core_ref, qkv_ref, out_ref, log_ref):
    starts = half_starts(core_ref)
    full = in_order(qkv_ref, starts)
    keys = full[:, PAIR : 2 * PAIR]
    values_t = full[:, 2 * PAIR :].T
    keep = causal_keep()
    for step in range(LEN // BLOCK):
        seen = (step + 1) * BLOCK
        queries = split_heads(full[step * BLOCK : seen, :PAIR])
        scores = dot32(keys[:seen], queries, ROWS_ROWS)
        last = jnp.where(keep, scores[seen - BLOCK :], -1e30)
        scores = jnp.concatenate([scores[: seen - BLOCK], last], axis=0) if step else last
        top = jnp.max(scores, axis=0, keepdims=True) * SCORE_SCALE
        exponent = jnp.exp2(scores * SCORE_SCALE - top)
        total = jnp.sum(exponent, axis=0, keepdims=True)
        low = exponent.astype(jnp.bfloat16)
        inverse = 1.0 / total
        logs = top + jnp.log2(total)
        parts = []
        for head in range(2):
            columns = slice(head * BLOCK, (head + 1) * BLOCK)
            attended = dot32(
                values_t[head * HEAD_DIM : (head + 1) * HEAD_DIM, :seen], low[:, columns]
            )
            parts.append(attended * inverse[:, columns])
            log_ref[0, head : head + 1, step * BLOCK : seen] = logs[:, columns]
        out_ref[block_rows(starts, step), :] = (
            jnp.concatenate(parts, axis=0).T.astype(jnp.bfloat16)
        )


def attend_backward_kernel(core_ref, qkv_ref, out_ref, log_ref, grad_ref, dqkv_ref, dk_ref, dv_ref):
    starts = half_starts(core_ref)
    full = in_order(qkv_ref, starts)
    out_grad = in_order(grad_ref, starts)
    attended = in_order(out_ref, starts)
    keys = full[:, PAIR : 2 * PAIR]
    values = full[:, 2 * PAIR :]
    keys_t = keys.T
    product_t = (out_grad.astype(jnp.float32) * attended.astype(jnp.float32)).T
    deltas = [
        jnp.sum(product_t[head * HEAD_DIM : (head + 1) * HEAD_DIM], axis=0, keepdims=True)
        for head in range(2)
    ]
    keep = causal_keep()
    factor = HEAD_DIM**-0.5
    steps = LEN // BLOCK
    for step in reversed(range(steps)):
        seen = (step + 1) * BLOCK
        columns = slice(step * BLOCK, seen)
        queries = split_heads(full[columns, :PAIR])
        grads = split_heads(out_grad[columns])
        logs = jnp.concatenate([log_ref[0, 0:1, columns], log_ref[0, 1:2, columns]], axis=1)
        delta = jnp.concatenate([deltas[0][:, columns], deltas[1][:, columns]], axis=1)
        scores = dot32(keys[:seen], queries, ROWS_ROWS)
        weights = jnp.exp2(scores * SCORE_SCALE - logs)
        last = jnp.where(keep, weights[seen - BLOCK :], 0.0)
        weights = jnp.concatenate([weights[: seen - BLOCK], last], axis=0) if step else last
        weight_grad = dot32(values[:seen], grads, ROWS_ROWS)
        value_term = dot32(weights.astype(jnp.bfloat16), grads)
        score_grad = (weights * (weight_grad - delta)).astype(jnp.bfloat16)
        key_term = dot32(score_grad, queries)
        if step == steps - 1:
            dk_ref[...] = key_term
            dv_ref[...] = value_term
        else:
            dk_ref[:seen, :] += key_term
            dv_ref[:seen, :] += value_term
        parts = [
            dot32(
                keys_t[head * HEAD_DIM : (head + 1) * HEAD_DIM, :seen],
                score_grad[:, head * BLOCK : (head + 1) * BLOCK],
            )
            for head in range(2)
        ]
        query_grad = jnp.concatenate(parts, axis=0).T * factor
        dqkv_ref[block_rows(starts, step), :PAIR] = query_grad.astype(jnp.bfloat16)
    half = LEN // 2
    for at, start in enumerate(starts):
        rows = slice(at * half, (at + 1) * half)
        dqkv_ref[pl.ds(start, half), PAIR : 2 * PAIR] = (dk_ref[rows, :] * factor).astype(
            jnp.bfloat16
        )
        dqkv_ref[pl.ds(start, half), 2 * PAIR :] = dv_ref[rows, :].astype(jnp.bfloat16)


def pair_block(width):
    return pl.BlockSpec((LEN, width), lambda pair, core: (0, pair))


LOG_BLOCK = pl.BlockSpec((1, 8, LEN), lambda pair, core: (pair, 0, 0))
KERNEL_PARAMS = pltpu.CompilerParams(vmem_limit_bytes=40 * 1024 * 1024)


def attend_forward(core, qkv):
    pairs = qkv.shape[1] // (3 * PAIR)
    return pl.pallas_call(
        attend_forward_kernel,
        grid_spec=pltpu.PrefetchScalarGridSpec(
            num_scalar_prefetch=1,
            grid=(pairs,),
            in_specs=[pair_block(3 * PAIR)],
            out_specs=[pair_block(PAIR), LOG_BLOCK],
        ),
        out_shape=[
            jax.ShapeDtypeStruct((LEN, pairs * PAIR), jnp.bfloat16),
            jax.ShapeDtypeStruct((pairs, 8, LEN), jnp.float32),
        ],
        compiler_params=KERNEL_PARAMS,
        cost_estimate=pl.CostEstimate(
            flops=pairs * 5 * LEN * LEN * PAIR,
            bytes_accessed=pairs * LEN * PAIR * 8,
            transcendentals=pairs * LEN * LEN,
        ),
        name="attend_forward",
    )(core, qkv)


def attend_backward(core, qkv, attended, logs, out_grad):
    pairs = qkv.shape[1] // (3 * PAIR)
    return pl.pallas_call(
        attend_backward_kernel,
        grid_spec=pltpu.PrefetchScalarGridSpec(
            num_scalar_prefetch=1,
            grid=(pairs,),
            in_specs=[pair_block(3 * PAIR), pair_block(PAIR), LOG_BLOCK, pair_block(PAIR)],
            out_specs=pair_block(3 * PAIR),
            scratch_shapes=[
                pltpu.VMEM((LEN, PAIR), jnp.float32),
                pltpu.VMEM((LEN, PAIR), jnp.float32),
            ],
        ),
        out_shape=jax.ShapeDtypeStruct(qkv.shape, jnp.bfloat16),
        compiler_params=KERNEL_PARAMS,
        cost_estimate=pl.CostEstimate(
            flops=pairs * 14 * LEN * LEN * PAIR,
            bytes_accessed=pairs * LEN * PAIR * 16,
            transcendentals=pairs * LEN * LEN,
        ),
        name="attend_backward",
    )(core, qkv, attended, logs, out_grad)


def local(
    tokens,
    ln1_gain,
    ln1_shift,
    qkv_weight,
    qv_bias,
    out_weight,
    out_bias,
    ln2_gain,
    ln2_shift,
    fc_weight,
    fc_bias,
    proj_weight,
    proj_bias,
    cotangent,
):
    size = lax.axis_size("tensor")
    place = lax.axis_index("tensor")
    near = [(i, i ^ 1) for i in range(size)]
    far = [(i, (i + size // 2) % size) for i in range(size)]
    core = (place % 2).astype(jnp.int32).reshape(1)
    own_rows, d = tokens.shape
    width = qkv_weight.shape[2]
    hidden_width = fc_weight.shape[1]
    assert size == 4 and 2 * own_rows == LEN

    def from_near(value):
        return lax.ppermute(value, "tensor", near)

    def from_far(value):
        return lax.ppermute(value, "tensor", far)

    biases = jnp.concatenate([qv_bias.reshape(-1), fc_bias])
    far_biases = from_far(biases)
    far_qkv = from_far(qkv_weight)
    far_out = from_far(out_weight)
    far_fc = from_far(fc_weight)
    far_proj = from_far(proj_weight)
    near_cotangent = from_near(cotangent)

    tok_rows = tokens.astype(jnp.float32)
    normed1, scale1 = normalize(tok_rows)
    first_own = (normed1 * ln1_gain + ln1_shift).astype(jnp.bfloat16)
    first = jnp.concatenate([first_own, from_near(first_own)], axis=0)

    pairs = 2 * width // PAIR
    qkv_both = jnp.concatenate([qkv_weight, far_qkv], axis=2)
    qkv_flat = qkv_both.reshape(3, d, pairs, PAIR).transpose(1, 2, 0, 3).reshape(d, -1)
    far_qv = far_biases[: 2 * width].reshape(2, width)
    qv_both = jnp.concatenate([qv_bias, far_qv], axis=1).reshape(2, pairs, PAIR)
    qkv_shift = jnp.stack([qv_both[0], jnp.zeros_like(qv_both[0]), qv_both[1]], axis=1).reshape(-1)
    qkv = (dot32(first, qkv_flat) + qkv_shift).astype(jnp.bfloat16)
    attended, logs = attend_forward(core, qkv)

    out_both = jnp.concatenate([out_weight, far_out], axis=0)
    branch_far = from_near(dot32(attended[own_rows:], out_both).astype(jnp.bfloat16))
    branch = dot32(attended[:own_rows], out_both) + branch_far.astype(jnp.float32)
    resid = tok_rows + branch + out_bias
    normed2, scale2 = normalize(resid)
    second_own = (normed2 * ln2_gain + ln2_shift).astype(jnp.bfloat16)
    second = jnp.concatenate([second_own, from_near(second_own)], axis=0)

    fc_both = jnp.concatenate([fc_weight, far_fc], axis=1)
    fc_shift = jnp.concatenate([fc_bias, far_biases[2 * width :]])
    proj_both = jnp.concatenate([proj_weight, far_proj], axis=0)
    hidden = dot32(second, fc_both) + fc_shift
    active, gelu_back = jax.vjp(partial(jax.nn.gelu, approximate=True), hidden)
    active_low = active.astype(jnp.bfloat16)
    mlp_far = from_near(dot32(active_low[own_rows:], proj_both).astype(jnp.bfloat16))
    mlp_out = dot32(active_low[:own_rows], proj_both) + mlp_far.astype(jnp.float32)
    output = (resid + mlp_out + proj_bias).astype(jnp.bfloat16)

    grad_rows = cotangent.astype(jnp.float32)
    proj_bias_grad = jnp.sum(grad_rows, axis=0)
    grad_full = jnp.concatenate([cotangent, near_cotangent], axis=0)
    active_grad = dot32(grad_full, proj_both, ROWS_ROWS)
    hidden_low = gelu_back(active_grad)[0].astype(jnp.bfloat16)
    second_far = from_near(
        dot32(hidden_low[own_rows:], fc_both, ROWS_ROWS).astype(jnp.bfloat16)
    )
    second_grad = dot32(hidden_low[:own_rows], fc_both, ROWS_ROWS) + second_far.astype(jnp.float32)

    columns_columns = (((0,), (0,)), ((), ()))

    def summed(own, other):
        return lax.psum((own + other.astype(jnp.float32)).astype(jnp.bfloat16), "dp").astype(
            jnp.float32
        )

    proj_far = from_far(
        dot32(active_low[:, hidden_width:], grad_full, columns_columns).astype(jnp.bfloat16)
    )
    proj_own = dot32(active_low[:, :hidden_width], grad_full, columns_columns)
    proj_weight_grad = summed(proj_own, proj_far)
    fc_far = from_far(
        dot32(second, hidden_low[:, hidden_width:], columns_columns).astype(jnp.bfloat16)
    )
    fc_own = dot32(second, hidden_low[:, :hidden_width], columns_columns)
    fc_weight_grad = summed(fc_own, fc_far)
    fc_sums = jnp.sum(hidden_low, axis=0, dtype=jnp.float32)

    resid_grad = grad_rows + norm_back(second_grad, normed2, scale2, ln2_gain)
    branch_low = resid_grad.astype(jnp.bfloat16)
    branch_full = jnp.concatenate([branch_low, from_near(branch_low)], axis=0)
    ln2_gain_grad = jnp.sum(second_grad * normed2, axis=0)
    ln2_shift_grad = jnp.sum(second_grad, axis=0)
    out_bias_grad = jnp.sum(branch_low, axis=0, dtype=jnp.float32)
    heads_grad = dot32(branch_full, out_both, ROWS_ROWS).astype(jnp.bfloat16)
    out_far = from_far(
        dot32(attended[:, width:], branch_full, columns_columns).astype(jnp.bfloat16)
    )
    out_own = dot32(attended[:, :width], branch_full, columns_columns)
    out_weight_grad = summed(out_own, out_far)

    qkv_grad = attend_backward(core, qkv, attended, logs, heads_grad)
    qkv_sums = jnp.sum(qkv_grad, axis=0, dtype=jnp.float32).reshape(pairs, 3, PAIR)
    qv_sums = qkv_sums[:, 0::2].transpose(1, 0, 2).reshape(2, 2 * width)
    qkv_both_grad = dot32(first, qkv_grad, columns_columns)
    qkv_both_grad = qkv_both_grad.reshape(d, pairs, 3, PAIR).transpose(2, 0, 1, 3)
    qkv_both_grad = qkv_both_grad.reshape(3, d, 2 * width)
    qkv_far = from_far(qkv_both_grad[:, :, width:].astype(jnp.bfloat16))
    qkv_weight_grad = summed(qkv_both_grad[:, :, :width], qkv_far)

    first_far = from_near(dot32(qkv_grad[own_rows:], qkv_flat, ROWS_ROWS).astype(jnp.bfloat16))
    first_grad = dot32(qkv_grad[:own_rows], qkv_flat, ROWS_ROWS) + first_far.astype(jnp.float32)
    ln1_gain_grad = jnp.sum(first_grad * normed1, axis=0)
    ln1_shift_grad = jnp.sum(first_grad, axis=0)
    tokens_grad = resid_grad + norm_back(first_grad, normed1, scale1, ln1_gain)

    other = (place + size // 2) % size
    split = jnp.zeros((size, 2 * width + hidden_width), jnp.float32)
    for at, columns in ((place, slice(0, 1)), (other, slice(1, 2))):
        part = jnp.concatenate(
            [
                qv_sums.reshape(2, 2, width)[:, columns].reshape(-1),
                fc_sums.reshape(2, hidden_width)[columns].reshape(-1),
            ]
        )
        split = lax.dynamic_update_slice(split, part[None], (at, 0))
    whole = jnp.concatenate(
        [
            ln1_gain_grad,
            ln1_shift_grad,
            out_bias_grad,
            ln2_gain_grad,
            ln2_shift_grad,
            proj_bias_grad,
            split.reshape(-1),
        ]
    )
    whole = lax.psum(whole, ("dp", "tensor"))
    ln1_gain_grad, ln1_shift_grad, out_bias_grad, ln2_gain_grad, ln2_shift_grad, proj_bias_grad = (
        whole[at * d : (at + 1) * d] for at in range(6)
    )
    mine = lax.dynamic_index_in_dim(whole[6 * d :].reshape(size, -1), place, 0, keepdims=False)
    qv_bias_grad = mine[: 2 * width].reshape(2, width)
    fc_bias_grad = mine[2 * width :]
    return (
        output,
        tokens_grad,
        ln1_gain_grad,
        ln1_shift_grad,
        qkv_weight_grad,
        qv_bias_grad,
        out_weight_grad,
        out_bias_grad,
        ln2_gain_grad,
        ln2_shift_grad,
        fc_weight_grad,
        fc_bias_grad,
        proj_weight_grad,
        proj_bias_grad,
    )


def solution(mesh):
    return jax.shard_map(
        local,
        mesh=mesh,
        in_specs=(
            P(("dp", "tensor"), None),
            P(),
            P(),
            P(None, None, "tensor"),
            P(None, "tensor"),
            P("tensor", None),
            P(),
            P(),
            P(),
            P(None, "tensor"),
            P("tensor"),
            P("tensor", None),
            P(),
            P(("dp", "tensor"), None),
        ),
        out_specs=(
            P(("dp", "tensor"), None),
            P(("dp", "tensor"), None),
            P(),
            P(),
            P(None, None, "tensor"),
            P(None, "tensor"),
            P("tensor", None),
            P(),
            P(),
            P(),
            P(None, "tensor"),
            P("tensor"),
            P("tensor", None),
            P(),
        ),
        check_vma=False,
    )
```

time: 736 us -> 360 us (0.49); the launches traced: 727 us -> 359 us
  waiting for transfers between devices: 401 us -> 187 us
  matrix products: 149 us -> 49.5 us
  other arithmetic: 53.9 us -> 18.7 us
  local copies, waits for them, and re-layouts: 33.3 us -> 12.3 us
  Pallas kernels: 0 us -> 19.4 us
  blocking collectives: 62.6 us -> 44.9 us
    psum x1, waiting for transfers between devices: 194 us -> 79.8 us  [summed(): lax.psum((own + other.astype(jnp.float32)).astype(jnp.bfloat16), 'dp')]
    all_gather x4 -> x0, waiting for transfers between devices: 110 us -> none  [the longest x1 31.2 us: local(): first_full = lax.all_gather(first_low, 'tensor', axis=0, tiled=True)]
    ppermute x0 -> x17, waiting for transfers between devices: none -> 107 us  [the longest x9 107 us: from_far(): return lax.ppermute(value, 'tensor', far)]
    dot_general x26 -> x19, matrix products: 149 us -> 49.5 us  [dot32(): lax.dot_general(left, right, dims, preferred_element_type=jnp.float32)]
    reduce_scatter x4 -> x0, waiting for transfers between devices: 96.8 us -> none  [the longest x1 37.8 us: local(): lax.psum_scatter(jnp.dot(heads_flat, out_weight, preferred_element_type=j...]
    reduce_sum x5 -> x1, other arithmetic: 19.8 us -> 0.39 us  [local(): jnp.sum(qkv_grad, axis=0, dtype=jnp.float32).reshape(pairs, 3, PAIR)]
    pallas_call x0 -> x2, Pallas kernels: none -> 19.4 us  [the longest x1 11.4 us: attend_backward(): pl.pallas_call(attend_backward_kernel, grid_spec=pltpu.PrefetchScalarGrid...]
    psum x2 -> x1, blocking collectives: 62.6 us -> 44.9 us  [local(): whole = lax.psum(whole, ('dp', 'tensor'))]
  transfers between devices with their start and end apart: 9 -> 18, of which waited for: 8 -> 8; matrix products, arithmetic and copies ran while one was open for 5% -> 15% of each run, Pallas kernels for 0% -> 3%
where the time goes in v1:
time: 360 us; the launch traced here: 359 us
  waiting for transfers between devices  187 us (52%)
  matrix products  49.5 us (14%)
  blocking collectives  44.9 us (12%)
  Pallas kernels  19.4 us (5%)
  other arithmetic  18.7 us (5%)
  between operations  14.7 us (4%)
  starting transfers between devices  12.5 us (3%)
  local copies, waits for them, and re-layouts  12.3 us (3%)
    ppermute x9, waiting for transfers between devices, from_far(): return lax.ppermute(value, 'tensor', far)  107 us
    psum x1, waiting for transfers between devices, summed(): lax.psum((own + other.astype(jnp.float32)).astype(jnp.bfloat16), 'dp')  79.8 us
    dot_general x19, matrix products, dot32(): lax.dot_general(left, right, dims, preferred_element_type=jnp.float32)  49.5 us
    psum x1, blocking collectives, local(): whole = lax.psum(whole, ('dp', 'tensor'))  44.9 us
    ppermute x9, starting transfers between devices, from_far(): return lax.ppermute(value, 'tensor', far)  11.5 us
    pallas_call x1, Pallas kernels, attend_backward(): pl.pallas_call(attend_backward_kernel, grid_spec=pltpu.PrefetchScalarGrid...  11.4 us
    pallas_call x1, Pallas kernels, attend_forward(): pl.pallas_call(attend_forward_kernel, grid_spec=pltpu.PrefetchScalarGridS...  8.03 us
  transfers between devices with their start and end apart: 18, of which 8 were waited for; matrix products, arithmetic and copies ran while one was open for 15% of the time, Pallas kernels for 3%

profile of v1, /device:TPU:0, one launch (start us, length us, event | category | flops | bytes accessed | tf_op | source)
XLA Modules:
  0.0 359.0 jit_solution(3578372415252918505)
XLA Ops:
  7.3 3.0 collective-permute-start.1
  14.8 1.9 collective-permute-start.3
  16.7 14.5 %collective-permute-done.2 = f32[1152]{0:T(1024)S(1)} collective-permute-done((f32[1152]{0:T(1024)S(1)}, f32[1152]{0:T(1024)S(1)}, u32[]{:S(2)}, u32[]{:S(2)}) %collective-permute-start.2) | collective-permute-done | bytes 4640 | tf_op jit(solution)/shard_map/ppermute | solution.py:247
  31.5 5.3 %collective-permute-done.3 = bf16[192,768]{1,0:T(8,128)(2,1)} collective-permute-done((bf16[192,768]{1,0:T(8,128)(2,1)S(1)}, bf16[192,768]{1,0:T(8,128)(2,1)}, u32[]{:S(2)}, u32[]{:S(2)}) %collective-permute-start.3) | collective-permute-done | bytes 294944 | tf_op jit(solution)/shard_map/ppermute | solution.py:247
  38.1 4.2 %add_convert_fusion.qkv_ref = bf16[1024,1152]{1,0:T(8,128)(2,1)S(1)} fusion(bf16[768,1152]{0,1:T(8,128)(2,1)S(1)} %bitcast.33, f32[1152]{0:T(1024)S(1)} %add.141, bf16[512,768]{1,0:T(8,128)(2,1)} %collective-permute-done, bf16[512,768]{1,0:T(8,128)(2,1)} %fusion.15), kind=kOutput, calls=%fused_computation.12 | convolution fusion | flops 1817444352 | bytes 5706240 | tf_op jit(solution)/shard_map/dot_general | solution.py:38
  42.3 8.0 %attend_forward.1 = (bf16[1024,384]{1,0:T(8,128)(2,1)S(1)}, f32[3,8,1024]{2,1,0:T(8,128)S(1)}) custom-call(s32[1]{0:T(128)} %bitcast.core_ref, bf16[1024,1152]{1,0:T(8,128)(2,1)S(1)} %add_convert_fusion.qkv_ref), custom_call_target="tpu_custom_call" | custom-call | flops 2013265920 | bytes 3145728 | tf_op jit(solution)/shard_map/attend_forward/pallas_call | solution.py:170
  51.9 1.7 collective-permute-start.6
  55.3 1.9 fusion.85
  61.4 19.5 %collective-permute-done.6 = bf16[768,768]{1,0:T(8,128)(2,1)} collective-permute-done((bf16[768,768]{1,0:T(8,128)(2,1)}, bf16[768,768]{1,0:T(8,128)(2,1)}, u32[]{:S(2)}, u32[]{:S(2)}) %collective-permute-start.6) | collective-permute-done | bytes 1179680 | tf_op jit(solution)/shard_map/ppermute | solution.py:247
  82.3 23.5 %collective-permute-done.7 = bf16[768,768]{1,0:T(8,128)(2,1)} collective-permute-done((bf16[768,768]{1,0:T(8,128)(2,1)}, bf16[768,768]{1,0:T(8,128)(2,1)}, u32[]{:S(2)}, u32[]{:S(2)}) %collective-permute-start.7) | collective-permute-done | bytes 1179680 | tf_op jit(solution)/shard_map/ppermute | solution.py:247
  107.2 2.6 fusion.68
  109.8 8.0 %convert_reduce_fusion = (f32[1536]{0:T(1024)S(1)}, bf16[1024,1536]{1,0:T(8,128)(2,1)S(1)}, bf16[1024,1536]{1,0:T(8,128)(2,1)S(1)}) fusion(f32[1024,1536]{1,0:T(8,128)S(1)} %fusion.68, f32[1536]{0:T(1024)S(1)} %pad_maximum_fusion.13, bf16[1024,768]{1,0:T(8,128)(2,1)S(1)} %constant_dynamic-update-slice_fusion.6, ...), kind=kOutput, calls=%fused_computation.9 | convolution fusion | flops 2455239168 | bytes 16527360 | tf_op jit(solution)/shard_map/dot_general | solution.py:38
  120.8 1.8 collective-permute-start.16
  122.6 2.3 fusion.53
  124.9 1.9 multiply_reduce_fusion
  126.8 1.9 convert_reduce_fusion.4
  130.8 18.8 %collective-permute-done.16 = bf16[768,768]{1,0:T(8,128)(2,1)S(1)} collective-permute-done((bf16[768,768]{1,0:T(8,128)(2,1)S(1)}, bf16[768,768]{1,0:T(8,128)(2,1)S(1)}, u32[]{:S(2)}, u32[]{:S(2)}) %collective-permute-start.16) | collective-permute-done | bytes 1179680 | tf_op jit(solution)/shard_map/ppermute | solution.py:247
  149.6 2.6 add_convert_fusion.1
  153.9 11.4 %attend_backward.1 = bf16[1024,1152]{1,0:T(8,128)(2,1)S(1)} custom-call(s32[1]{0:T(128)} %bitcast.core_ref, bf16[1024,1152]{1,0:T(8,128)(2,1)S(1)} %copy-done.1, bf16[1024,384]{1,0:T(8,128)(2,1)S(1)} %get-tuple-element.16.out_ref, f32[3,8,1024]{2,1,0:T(8,128)S(1)} %get-tuple-element.17.log_ref, bf16[1024,384]{1,0:T(8,128)(2,1)S(1)} %convolution_convert_fusion.grad_ref), custom_call_target="tpu_custom_call" | custom-call | flops 5637144576 | bytes 6291456 | tf_op jit(solution)/shard_map/attend_backward/pallas_call | solution.py:194
  165.3 3.5 fusion.65
  169.2 1.8 collective-permute-start.13
  172.0 3.0 collective-permute-done.15
  174.9 2.5 add_convert_fusion.2
  177.4 22.4 %collective-permute-done.14 = bf16[192,768]{1,0:T(8,128)(2,1)S(1)} collective-permute-done((bf16[192,768]{1,0:T(8,128)(2,1)S(1)}, bf16[192,768]{1,0:T(8,128)(2,1)S(1)}, u32[]{:S(2)}, u32[]{:S(2)}) %collective-permute-start.14) | collective-permute-done | bytes 294944 | tf_op jit(solution)/shard_map/ppermute | solution.py:247
  202.3 3.7 %convolution_convert_fusion.1 = bf16[512,768]{1,0:T(8,128)(2,1)} fusion(bf16[768,1152]{0,1:T(8,128)(2,1)} %bitcast.34, bf16[1024,1152]{1,0:T(8,128)(2,1)S(1)} %attend_backward.1), kind=kOutput, calls=%fused_computation.72 | convolution fusion | flops 906362880 | bytes 3735552 | tf_op jit(solution)/shard_map/dot_general | solution.py:38
  206.0 3.4 add_convert_fusion.3
  210.7 4.3 %fusion.20 = (f32[768]{0:T(1024)S(1)}, f32[512]{0:T(512)S(1)}, f32[512]{0:T(512)S(1)}, f32[768]{0:T(1024)S(1)}, f32[512,768]{1,0:T(8,128)}) fusion(bf16[512,768]{1,0:T(8,128)(2,1)S(1)} %copy-done.5, f32[512]{0:T(512)S(1)} %add_rsqrt_fusion.1, f32[512]{0:T(512)S(1)} %broadcast_multiply_fusion.5, f32[768]{0:T(1024)S(1)} %copy-done.15, ...), kind=kOutput, calls=%fused_computation.36 | convolution fusion | flops 910685696 | bytes 6113280 | tf_op jit(solution)/shard_map/dot_general | solution.py:38
  215.1 44.9 %psum.35 = f32[9216]{0:T(1024)S(1)} all-reduce(f32[9216]{0:T(1024)S(1)} %constant_dynamic-update-slice_fusion.10), channel_id=1, replica_groups=mesh['dp'=8,'tensor'=4] {'dp','tensor'}, use_global_device_ids=true, to_apply=%region_16.17 | all-reduce | flops 9216 | bytes 73728 | tf_op jit(solution)/shard_map/psum | solution.py:367
  262.0 3.6 fusion.19
  265.6 79.8 %all-reduce.3.cloned.1.call-done = (bf16[3,768,192]{1,2,0:T(8,128)(2,1)}, bf16[192,768]{1,0:T(8,128)(2,1)}, bf16[768,768]{1,0:T(8,128)(2,1)}, bf16[768,768]{1,0:T(8,128)(2,1)}) async-done(((bf16[3,768,192]{1,2,0:T(8,128)(2,1)}, bf16[192,768]{1,0:T(8,128)(2,1)}, bf16[768,768]{1,0:T(8,128)(2,1)}, bf16[768,768]{1,0:T(8,128)(2,1)}), (bf16[3,768,192]{1,2,0:T(8,128)(2,1)}, bf16[192,768]{1,0:T(8,128)(2,1)}, ...) | async-done | bytes 3538960 | tf_op jit(solution)/shard_map/psum | solution.py:302
  345.4 2.9 convert_element_type.140
  348.3 1.6 convert_element_type.144
  (150 shorter events, 32.1 us)
Async XLA Ops:
  7.2 6.0 %copy-start.4 = (bf16[512,768]{1,0:T(8,128)(2,1)S(1)}, bf16[512,768]{1,0:T(8,128)(2,1)}, u32[]{:S(2)}) copy-start(bf16[512,768]{1,0:T(8,128)(2,1)} %param.14) | copy-start | bytes 2359300
  7.2 6.0 %copy-start.15 = (f32[768]{0:T(1024)S(1)}, f32[768]{0:T(1024)}, u32[]{:S(2)}) copy-start(f32[768]{0:T(1024)} %param.15) | copy-start | bytes 9220
  7.2 6.0 %copy-start.19 = (f32[768]{0:T(1024)S(1)}, f32[768]{0:T(1024)}, u32[]{:S(2)}) copy-start(f32[768]{0:T(1024)} %param.16) | copy-start | bytes 9220
  7.2 7.2 %copy-start.18 = (f32[2,192]{1,0:T(2,128)S(1)}, f32[2,192]{1,0:T(2,128)}, u32[]{:S(2)}) copy-start(f32[2,192]{1,0:T(2,128)} %param.18) | copy-start | bytes 4612
  7.2 7.3 %copy-start.16 = (f32[768]{0:T(1024)S(1)}, f32[768]{0:T(1024)}, u32[]{:S(2)}) copy-start(f32[768]{0:T(1024)} %param.24) | copy-start | bytes 9220
  7.2 7.5 %copy-start.14 = (bf16[192,768]{1,0:T(8,128)(2,1)S(1)}, bf16[192,768]{1,0:T(8,128)(2,1)}, u32[]{:S(2)}) copy-start(bf16[192,768]{1,0:T(8,128)(2,1)} %param.19) | copy-start | bytes 884740
  7.2 338.1 %all-reduce.3.cloned.1.call-start = ((), (), s32[]{:S(2)}) async-start(), calls=%async_computation | async-start | bytes 7077888 | tf_op jit(solution)/shard_map/psum | solution.py:302
  7.3 30.5 %collective-permute-start.1 = (bf16[3,768,192]{1,2,0:T(8,128)(2,1)}, bf16[3,768,192]{1,2,0:T(8,128)(2,1)S(1)}, u32[]{:S(2)}, u32[]{:S(2)}) collective-permute-start(bf16[3,768,192]{1,2,0:T(8,128)(2,1)} %param.17), channel_id=1, source_target_pairs={{0,2},{1,3},{2,0},{3,1},{4,6},{5,7},{6,4},{7,5},{8,10},{9,11},{10,... | collective-permute-start | bytes 2654216 | tf_op jit(solution)/shard_map/ppermute | solution.py:247
  13.1 24.6 %copy-start.9 = (bf16[3,768,192]{1,2,0:T(8,128)(2,1)S(1)}, bf16[3,768,192]{1,2,0:T(8,128)(2,1)}, u32[]{:S(2)}) copy-start(bf16[3,768,192]{1,2,0:T(8,128)(2,1)} %param.17) | copy-start | bytes 2654212
  14.4 23.6 %collective-permute-start = (bf16[512,768]{1,0:T(8,128)(2,1)}, bf16[512,768]{1,0:T(8,128)(2,1)}, u32[]{:S(2)}, u32[]{:S(2)}) collective-permute-start(bf16[512,768]{1,0:T(8,128)(2,1)} %fusion.15), channel_id=1, source_target_pairs={{0,1},{1,0},{2,3},{3,2},{4,5},{5,4},{6,7},{7,6},{8,9},{9,8},{10,11... | collective-permute-start | bytes 2359304 | tf_op jit(solution)/shard_map/ppermute | solution.py:244
  14.5 16.7 %collective-permute-start.2 = (f32[1152]{0:T(1024)S(1)}, f32[1152]{0:T(1024)S(1)}, u32[]{:S(2)}, u32[]{:S(2)}) collective-permute-start(f32[1152]{0:T(1024)S(1)} %pad_maximum_fusion.12), channel_id=1, source_target_pairs={{0,2},{1,3},{2,0},{3,1},{4,6},{5,7},{6,4},{7,5},{8,10},{9,11},{10,... | collective-permute-start | bytes 13832 | tf_op jit(solution)/shard_map/ppermute | solution.py:247
  14.8 22.0 %collective-permute-start.3 = (bf16[192,768]{1,0:T(8,128)(2,1)S(1)}, bf16[192,768]{1,0:T(8,128)(2,1)}, u32[]{:S(2)}, u32[]{:S(2)}) collective-permute-start(bf16[192,768]{1,0:T(8,128)(2,1)S(1)} %copy-done.14), channel_id=1, source_target_pairs={{0,2},{1,3},{2,0},{3,1},{4,6},{5,7},{6,4},{7,5},{8,10},{9,11},{10,... | collective-permute-start | bytes 884744 | tf_op jit(solution)/shard_map/ppermute | solution.py:247
  38.0 4.3 %copy-start.7 = (bf16[768,3,3,128]{0,3,2,1:T(8,128)(2,1)}, bf16[768,3,3,128]{0,3,2,1:T(8,128)(2,1)S(1)}, u32[]{:S(2)}) copy-start(bf16[768,3,3,128]{0,3,2,1:T(8,128)(2,1)S(1)} %copy.31) | copy-start | bytes 5308420
  42.3 8.1 %copy-start = (bf16[1024,1152]{1,0:T(8,128)(2,1)}, bf16[1024,1152]{1,0:T(8,128)(2,1)S(1)}, u32[]{:S(2)}) copy-start(bf16[1024,1152]{1,0:T(8,128)(2,1)S(1)} %add_convert_fusion.qkv_ref) | copy-start | bytes 7077892
  51.9 3.4 collective-permute-start.4
  51.9 29.1 %collective-permute-start.6 = (bf16[768,768]{1,0:T(8,128)(2,1)}, bf16[768,768]{1,0:T(8,128)(2,1)}, u32[]{:S(2)}, u32[]{:S(2)}) collective-permute-start(bf16[768,768]{1,0:T(8,128)(2,1)} %param.23), channel_id=1, source_target_pairs={{0,2},{1,3},{2,0},{3,1},{4,6},{5,7},{6,4},{7,5},{8,10},{9,11},{10,... | collective-permute-start | bytes 3538952 | tf_op jit(solution)/shard_map/ppermute | solution.py:247
  53.6 52.2 %collective-permute-start.7 = (bf16[768,768]{1,0:T(8,128)(2,1)}, bf16[768,768]{1,0:T(8,128)(2,1)}, u32[]{:S(2)}, u32[]{:S(2)}) collective-permute-start(bf16[768,768]{1,0:T(8,128)(2,1)} %param.25), channel_id=1, source_target_pairs={{0,2},{1,3},{2,0},{3,1},{4,6},{5,7},{6,4},{7,5},{8,10},{9,11},{10,... | collective-permute-start | bytes 3538952 | tf_op jit(solution)/shard_map/ppermute | solution.py:247
  53.9 6.3 %collective-permute-start.9 = (bf16[512,768]{1,0:T(8,128)(2,1)S(1)}, bf16[512,768]{1,0:T(8,128)(2,1)}, u32[]{:S(2)}, u32[]{:S(2)}) collective-permute-start(bf16[512,768]{1,0:T(8,128)(2,1)S(1)} %copy-done.6), channel_id=1, source_target_pairs={{0,1},{1,0},{2,3},{3,2},{4,5},{5,4},{6,7},{7,6},{8,9},{9,8},{10,11... | collective-permute-start | bytes 2359304 | tf_op jit(solution)/shard_map/ppermute | solution.py:244
  57.1 69.7 %copy-start.2 = (f32[512,768]{1,0:T(8,128)}, f32[512,768]{1,0:T(8,128)S(1)}, u32[]{:S(2)}) copy-start(f32[512,768]{1,0:T(8,128)S(1)} %get-tuple-element.50) | copy-start | bytes 4718596
  58.2 49.0 %collective-permute-start.5 = (bf16[512,768]{1,0:T(8,128)(2,1)S(1)}, bf16[512,768]{1,0:T(8,128)(2,1)S(1)}, u32[]{:S(2)}, u32[]{:S(2)}) collective-permute-start(bf16[512,768]{1,0:T(8,128)(2,1)S(1)} %add_convert_fusion.4), channel_id=1, source_target_pairs={{0,1},{1,0},{2,3},{3,2},{4,5},{5,4},{6,7},{7,6},{8,9},{9,8},{10,11... | collective-permute-start | bytes 2359304 | tf_op jit(solution)/shard_map/ppermute | solution.py:244
  107.2 15.4 %copy-start.11 = (bf16[1536,768]{1,0:T(8,128)(2,1)}, bf16[1536,768]{1,0:T(8,128)(2,1)S(1)}, u32[]{:S(2)}) copy-start(bf16[1536,768]{1,0:T(8,128)(2,1)S(1)} %constant_dynamic-update-slice_fusion.4) | copy-start | bytes 7077892
  117.8 31.8 %copy-start.23 = (bf16[1024,1536]{1,0:T(8,128)(2,1)}, bf16[1024,1536]{1,0:T(8,128)(2,1)S(1)}, u32[]{:S(2)}) copy-start(bf16[1024,1536]{1,0:T(8,128)(2,1)S(1)} %get-tuple-element.39) | copy-start | bytes 9437188
  119.2 5.7 %collective-permute-start.10 = (bf16[512,768]{1,0:T(8,128)(2,1)S(1)}, bf16[512,768]{1,0:T(8,128)(2,1)S(1)}, u32[]{:S(2)}, u32[]{:S(2)}) collective-permute-start(bf16[512,768]{1,0:T(8,128)(2,1)S(1)} %fusion.56), channel_id=1, source_target_pairs={{0,1},{1,0},{2,3},{3,2},{4,5},{5,4},{6,7},{7,6},{8,9},{9,8},{10,11... | collective-permute-start | bytes 2359304 | tf_op jit(solution)/shard_map/ppermute | solution.py:244
  120.8 28.8 %collective-permute-start.16 = (bf16[768,768]{1,0:T(8,128)(2,1)S(1)}, bf16[768,768]{1,0:T(8,128)(2,1)S(1)}, u32[]{:S(2)}, u32[]{:S(2)}) collective-permute-start(bf16[768,768]{1,0:T(8,128)(2,1)S(1)} %fusion.42), channel_id=1, source_target_pairs={{0,2},{1,3},{2,0},{3,1},{4,6},{5,7},{6,4},{7,5},{8,10},{9,11},{10,... | collective-permute-start | bytes 3538952 | tf_op jit(solution)/shard_map/ppermute | solution.py:247
  128.7 23.5 %collective-permute-start.11 = (bf16[512,768]{1,0:T(8,128)(2,1)S(1)}, bf16[512,768]{1,0:T(8,128)(2,1)S(1)}, u32[]{:S(2)}, u32[]{:S(2)}) collective-permute-start(bf16[512,768]{1,0:T(8,128)(2,1)S(1)} %get-tuple-element.37), channel_id=1, source_target_pairs={{0,1},{1,0},{2,3},{3,2},{4,5},{5,4},{6,7},{7,6},{8,9},{9,8},{10,11... | collective-permute-start | bytes 2359304 | tf_op jit(solution)/shard_map/ppermute | solution.py:244
  130.4 44.5 %collective-permute-start.15 = (bf16[768,768]{1,0:T(8,128)(2,1)S(1)}, bf16[768,768]{1,0:T(8,128)(2,1)S(1)}, u32[]{:S(2)}, u32[]{:S(2)}) collective-permute-start(bf16[768,768]{1,0:T(8,128)(2,1)S(1)} %fusion.39), channel_id=1, source_target_pairs={{0,2},{1,3},{2,0},{3,1},{4,6},{5,7},{6,4},{7,5},{8,10},{9,11},{10,... | collective-permute-start | bytes 3538952 | tf_op jit(solution)/shard_map/ppermute | solution.py:247
  130.8 75.2 %collective-permute-start.8 = (bf16[512,768]{1,0:T(8,128)(2,1)}, bf16[512,768]{1,0:T(8,128)(2,1)}, u32[]{:S(2)}, u32[]{:S(2)}) collective-permute-start(bf16[512,768]{1,0:T(8,128)(2,1)} %fusion.53), channel_id=1, source_target_pairs={{0,1},{1,0},{2,3},{3,2},{4,5},{5,4},{6,7},{7,6},{8,9},{9,8},{10,11... | collective-permute-start | bytes 2359304 | tf_op jit(solution)/shard_map/ppermute | solution.py:244
  169.2 31.9 %collective-permute-start.13 = (bf16[3,768,192]{1,2,0:T(8,128)(2,1)S(1)}, bf16[3,768,192]{1,2,0:T(8,128)(2,1)S(1)}, u32[]{:S(2)}, u32[]{:S(2)}) collective-permute-start(bf16[3,768,192]{1,2,0:T(8,128)(2,1)S(1)} %slice.254), channel_id=1, source_target_pairs={{0,2},{1,3},{2,0},{3,1},{4,6},{5,7},{6,4},{7,5},{8,10},{9,11},{10,... | collective-permute-start | bytes 2654216 | tf_op jit(solution)/shard_map/ppermute | solution.py:247
  171.6 28.2 %collective-permute-start.14 = (bf16[192,768]{1,0:T(8,128)(2,1)S(1)}, bf16[192,768]{1,0:T(8,128)(2,1)S(1)}, u32[]{:S(2)}, u32[]{:S(2)}) collective-permute-start(bf16[192,768]{1,0:T(8,128)(2,1)S(1)} %convolution_convert_fusion.3), channel_id=1, source_target_pairs={{0,2},{1,3},{2,0},{3,1},{4,6},{5,7},{6,4},{7,5},{8,10},{9,11},{10,... | collective-permute-start | bytes 884744 | tf_op jit(solution)/shard_map/ppermute | solution.py:247
  202.3 3.7 %copy-start.3 = (f32[512,768]{1,0:T(8,128)S(1)}, f32[512,768]{1,0:T(8,128)}, u32[]{:S(2)}) copy-start(f32[512,768]{1,0:T(8,128)} %copy-done.2) | copy-start | bytes 4718596
  202.3 3.7 %copy-start.12 = (bf16[1536,768]{1,0:T(8,128)(2,1)S(1)}, bf16[1536,768]{1,0:T(8,128)(2,1)}, u32[]{:S(2)}) copy-start(bf16[1536,768]{1,0:T(8,128)(2,1)} %copy-done.11) | copy-start | bytes 7077892
  206.0 4.7 %collective-permute-start.12 = (bf16[512,768]{1,0:T(8,128)(2,1)}, bf16[512,768]{1,0:T(8,128)(2,1)}, u32[]{:S(2)}, u32[]{:S(2)}) collective-permute-start(bf16[512,768]{1,0:T(8,128)(2,1)} %convolution_convert_fusion.1), channel_id=1, source_target_pairs={{0,1},{1,0},{2,3},{3,2},{4,5},{5,4},{6,7},{7,6},{8,9},{9,8},{10,11... | collective-permute-start | bytes 2359304 | tf_op jit(solution)/shard_map/ppermute | solution.py:244
  (11 other events, 24.6 us)
Sparse Core Ops, SparseCore 0:
  202.4 142.9 all-reduce.2

commit v2 on v1

--- a/solution.py
+++ b/solution.py
@@ -214,6 +214,31 @@
     )(core, qkv, attended, logs, out_grad)
 
 
+def sum_over_dp(rows, bits):
+    place = lax.axis_index("dp")
+    size = lax.axis_size("dp")
+
+    def along(value, bit):
+        return lax.ppermute(value, "dp", [(i, i ^ (1 << bit)) for i in range(size)])
+
+    for bit in bits:
+        extent = rows.shape[0] // 2
+        upper = (place >> bit) & 1
+        kept = lax.dynamic_slice_in_dim(rows, upper * extent, extent, 0)
+        sent = lax.dynamic_slice_in_dim(rows, (1 - upper) * extent, extent, 0)
+        rows = (kept.astype(jnp.float32) + along(sent, bit).astype(jnp.float32)).astype(
+            jnp.bfloat16
+        )
+    for bit in reversed(bits):
+        other = along(rows, bit)
+        rows = jnp.where(
+            ((place >> bit) & 1) == 0,
+            jnp.concatenate([rows, other], axis=0),
+            jnp.concatenate([other, rows], axis=0),
+        )
+    return rows
+
+
 def local(
     tokens,
     ln1_gain,
@@ -248,16 +273,36 @@
 
     biases = jnp.concatenate([qv_bias.reshape(-1), fc_bias])
     far_biases = from_far(biases)
-    far_qkv = from_far(qkv_weight)
-    far_out = from_far(out_weight)
-    far_fc = from_far(fc_weight)
-    far_proj = from_far(proj_weight)
+    side = lax.axis_index("dp") % 2
+    beside = [(i, i ^ 1) for i in range(lax.axis_size("dp"))]
+
+    def from_beside(value):
+        return lax.ppermute(value, "dp", beside)
+
+    def ordered(got, handed, axis):
+        return jnp.where(
+            side == 0,
+            jnp.concatenate([got, handed], axis=axis),
+            jnp.concatenate([handed, got], axis=axis),
+        )
+
+    def half_of(value, axis):
+        extent = value.shape[axis] // 2
+        return lax.dynamic_slice_in_dim(value, side * extent, extent, axis)
+
+    qkv_half, far_biases = lax.optimization_barrier((half_of(qkv_weight, 1), far_biases))
+    got_qkv = from_far(qkv_half)
+    got_out = from_far(half_of(out_weight, 0))
+    got_fc = from_far(half_of(fc_weight, 0))
+    got_proj = from_far(half_of(proj_weight, 0))
+    far_qkv = ordered(got_qkv, from_beside(got_qkv), 1)
     near_cotangent = from_near(cotangent)
 
     tok_rows = tokens.astype(jnp.float32)
     normed1, scale1 = normalize(tok_rows)
     first_own = (normed1 * ln1_gain + ln1_shift).astype(jnp.bfloat16)
     first = jnp.concatenate([first_own, from_near(first_own)], axis=0)
+    first, got_fc = lax.optimization_barrier((first, got_fc))
 
     pairs = 2 * width // PAIR
     qkv_both = jnp.concatenate([qkv_weight, far_qkv], axis=2)
@@ -266,7 +311,12 @@
     qv_both = jnp.concatenate([qv_bias, far_qv], axis=1).reshape(2, pairs, PAIR)
     qkv_shift = jnp.stack([qv_both[0], jnp.zeros_like(qv_both[0]), qv_both[1]], axis=1).reshape(-1)
     qkv = (dot32(first, qkv_flat) + qkv_shift).astype(jnp.bfloat16)
+    handed_fc = from_beside(got_fc)
     attended, logs = attend_forward(core, qkv)
+    attended, handed_fc, got_proj = lax.optimization_barrier((attended, handed_fc, got_proj))
+    far_out = ordered(got_out, from_beside(got_out), 0)
+    far_fc = ordered(got_fc, handed_fc, 0)
+    handed_proj = from_beside(got_proj)
 
     out_both = jnp.concatenate([out_weight, far_out], axis=0)
     branch_far = from_near(dot32(attended[own_rows:], out_both).astype(jnp.bfloat16))
@@ -278,8 +328,9 @@
 
     fc_both = jnp.concatenate([fc_weight, far_fc], axis=1)
     fc_shift = jnp.concatenate([fc_bias, far_biases[2 * width :]])
-    proj_both = jnp.concatenate([proj_weight, far_proj], axis=0)
     hidden = dot32(second, fc_both) + fc_shift
+    hidden, got_proj, handed_proj = lax.optimization_barrier((hidden, got_proj, handed_proj))
+    proj_both = jnp.concatenate([proj_weight, ordered(got_proj, handed_proj, 0)], axis=0)
     active, gelu_back = jax.vjp(partial(jax.nn.gelu, approximate=True), hidden)
     active_low = active.astype(jnp.bfloat16)
     mlp_far = from_near(dot32(active_low[own_rows:], proj_both).astype(jnp.bfloat16))
@@ -298,21 +349,17 @@
 
     columns_columns = (((0,), (0,)), ((), ()))
 
-    def summed(own, other):
-        return lax.psum((own + other.astype(jnp.float32)).astype(jnp.bfloat16), "dp").astype(
-            jnp.float32
-        )
+    def joined(own, other):
+        return (own + other.astype(jnp.float32)).astype(jnp.bfloat16)
 
     proj_far = from_far(
         dot32(active_low[:, hidden_width:], grad_full, columns_columns).astype(jnp.bfloat16)
     )
     proj_own = dot32(active_low[:, :hidden_width], grad_full, columns_columns)
-    proj_weight_grad = summed(proj_own, proj_far)
     fc_far = from_far(
         dot32(second, hidden_low[:, hidden_width:], columns_columns).astype(jnp.bfloat16)
     )
     fc_own = dot32(second, hidden_low[:, :hidden_width], columns_columns)
-    fc_weight_grad = summed(fc_own, fc_far)
     fc_sums = jnp.sum(hidden_low, axis=0, dtype=jnp.float32)
 
     resid_grad = grad_rows + norm_back(second_grad, normed2, scale2, ln2_gain)
@@ -322,20 +369,27 @@
     ln2_shift_grad = jnp.sum(second_grad, axis=0)
     out_bias_grad = jnp.sum(branch_low, axis=0, dtype=jnp.float32)
     heads_grad = dot32(branch_full, out_both, ROWS_ROWS).astype(jnp.bfloat16)
-    out_far = from_far(
-        dot32(attended[:, width:], branch_full, columns_columns).astype(jnp.bfloat16)
-    )
-    out_own = dot32(attended[:, :width], branch_full, columns_columns)
-    out_weight_grad = summed(out_own, out_far)
+    out_both_grad = dot32(attended, branch_full, columns_columns)
 
     qkv_grad = attend_backward(core, qkv, attended, logs, heads_grad)
-    qkv_sums = jnp.sum(qkv_grad, axis=0, dtype=jnp.float32).reshape(pairs, 3, PAIR)
+    fc_own, proj_own, late_grad = lax.optimization_barrier((fc_own, proj_own, qkv_grad))
+    bits = range(lax.axis_size("dp").bit_length() - 1)
+    fc_weight_grad = sum_over_dp(joined(fc_own, fc_far), [*bits]).astype(jnp.float32)
+    proj_weight_grad = sum_over_dp(joined(proj_own, proj_far), [*bits][1:] + [0]).astype(
+        jnp.float32
+    )
+    qkv_sums = jnp.sum(late_grad, axis=0, dtype=jnp.float32).reshape(pairs, 3, PAIR)
     qv_sums = qkv_sums[:, 0::2].transpose(1, 0, 2).reshape(2, 2 * width)
-    qkv_both_grad = dot32(first, qkv_grad, columns_columns)
-    qkv_both_grad = qkv_both_grad.reshape(d, pairs, 3, PAIR).transpose(2, 0, 1, 3)
-    qkv_both_grad = qkv_both_grad.reshape(3, d, 2 * width)
-    qkv_far = from_far(qkv_both_grad[:, :, width:].astype(jnp.bfloat16))
-    qkv_weight_grad = summed(qkv_both_grad[:, :, :width], qkv_far)
+    qkv_both_grad = dot32(qkv_grad, first, columns_columns).reshape(pairs, 3, PAIR, d)
+    qkv_both_grad = qkv_both_grad.transpose(1, 0, 2, 3).reshape(3, 2, width, d)
+    last_far = from_far(
+        jnp.concatenate(
+            [qkv_both_grad[:, 1].reshape(3 * width, d), out_both_grad[width:]], axis=0
+        ).astype(jnp.bfloat16)
+    )
+    last_own = jnp.concatenate(
+        [qkv_both_grad[:, 0].reshape(3 * width, d), out_both_grad[:width]], axis=0
+    )
 
     first_far = from_near(dot32(qkv_grad[own_rows:], qkv_flat, ROWS_ROWS).astype(jnp.bfloat16))
     first_grad = dot32(qkv_grad[:own_rows], qkv_flat, ROWS_ROWS) + first_far.astype(jnp.float32)
@@ -343,17 +397,7 @@
     ln1_shift_grad = jnp.sum(first_grad, axis=0)
     tokens_grad = resid_grad + norm_back(first_grad, normed1, scale1, ln1_gain)
 
-    other = (place + size // 2) % size
-    split = jnp.zeros((size, 2 * width + hidden_width), jnp.float32)
-    for at, columns in ((place, slice(0, 1)), (other, slice(1, 2))):
-        part = jnp.concatenate(
-            [
-                qv_sums.reshape(2, 2, width)[:, columns].reshape(-1),
-                fc_sums.reshape(2, hidden_width)[columns].reshape(-1),
-            ]
-        )
-        split = lax.dynamic_update_slice(split, part[None], (at, 0))
-    whole = jnp.concatenate(
+    gains = jnp.concatenate(
         [
             ln1_gain_grad,
             ln1_shift_grad,
@@ -361,16 +405,35 @@
             ln2_gain_grad,
             ln2_shift_grad,
             proj_bias_grad,
-            split.reshape(-1),
         ]
     )
-    whole = lax.psum(whole, ("dp", "tensor"))
+    gains = gains + from_near(gains)
+    split = qv_sums.reshape(2, 2, width)
+    split_far = from_far(
+        jnp.concatenate([gains, split[:, 1].reshape(-1), fc_sums[hidden_width:]])
+    )
+    split_own = jnp.concatenate([gains, split[:, 0].reshape(-1), fc_sums[:hidden_width]])
+    small_part = split_own + split_far
+    edge = 4 * width
+    cut = edge * 2 // 3
+    short = -small_part.shape[0] % d
+    small_part = jnp.pad(small_part, (0, short)).reshape(-1, d)
+    small_rows = -(-small_part.shape[0] // 128) * 128
+    small_part = jnp.pad(small_part, ((0, small_rows - small_part.shape[0]), (0, 0)))
+    last_low = joined(last_own, last_far)
+    early = last_low[:cut]
+    late = jnp.concatenate([last_low[cut:], small_part.astype(jnp.bfloat16)], axis=0)
+    early = sum_over_dp(early, [*bits])
+    late = sum_over_dp(late, [*bits][1:] + [0])
+    qkv_low = jnp.concatenate([early, late], axis=0)[: 3 * width].reshape(3, width, d)
+    qkv_weight_grad = qkv_low.astype(jnp.float32).transpose(0, 2, 1)
+    out_weight_grad = late[3 * width - cut : edge - cut].astype(jnp.float32)
+    small = late[edge - cut :].astype(jnp.float32).reshape(-1)
     ln1_gain_grad, ln1_shift_grad, out_bias_grad, ln2_gain_grad, ln2_shift_grad, proj_bias_grad = (
-        whole[at * d : (at + 1) * d] for at in range(6)
-    )
-    mine = lax.dynamic_index_in_dim(whole[6 * d :].reshape(size, -1), place, 0, keepdims=False)
-    qv_bias_grad = mine[: 2 * width].reshape(2, width)
-    fc_bias_grad = mine[2 * width :]
+        small[at * d : (at + 1) * d] for at in range(6)
+    )
+    qv_bias_grad = small[6 * d : 6 * d + 2 * width].reshape(2, width)
+    fc_bias_grad = small[6 * d + 2 * width : 6 * d + 2 * width + hidden_width]
     return (
         output,
         tokens_grad,

time: 360 us -> 286 us (0.79); the launches traced: 359 us -> 281 us
  waiting for transfers between devices: 187 us -> 99.9 us
  blocking collectives: 44.9 us -> 0 us
  starting transfers between devices: 12.5 us -> 50.4 us
  other arithmetic: 18.7 us -> 37.1 us
  local copies, waits for them, and re-layouts: 12.3 us -> 25.2 us
  between operations: 14.7 us -> 2.02 us
    ppermute x9, waiting for transfers between devices: 107 us -> 18.5 us  [from_far(): return lax.ppermute(value, 'tensor', far)]
    psum x1 -> x0, waiting for transfers between devices: 79.8 us -> none  [summed(): lax.psum((own + other.astype(jnp.float32)).astype(jnp.bfloat16), 'dp')]
    ppermute x0 -> x28, waiting for transfers between devices: none -> 79.2 us  [the longest x24 65.7 us: along(): return lax.ppermute(value, 'dp', [(i, i ^ 1 << bit) for i in range(size)])]
    psum x1 -> x0, blocking collectives: 44.9 us -> none  [local(): whole = lax.psum(whole, ('dp', 'tensor'))]
    ppermute x0 -> x28, starting transfers between devices: none -> 37.3 us  [the longest x24 33.2 us: along(): return lax.ppermute(value, 'dp', [(i, i ^ 1 << bit) for i in range(size)])]
    convert_element_type x5 -> x20, other arithmetic: 7.91 us -> 15 us  [the longest x3 5.71 us: joined(): return (own + other.astype(jnp.float32)).astype(jnp.bfloat16)]
    slice x8 -> x12, local copies, waits for them, and re-layouts: 1.46 us -> 8.44 us  [the longest x1 1.92 us: local(): out_both_grad[:width]]
    select_n x0 -> x14, other arithmetic: none -> 6.91 us  [the longest x4 5.76 us: ordered(): jnp.where(side == 0, jnp.concatenate([got, handed], axis=axis), jnp.conca...]
  transfers between devices with their start and end apart: 18 -> 46, of which waited for: 8 -> 19; matrix products, arithmetic and copies ran while one was open for 15% -> 31% of each run, Pallas kernels for 3% -> 7%
where the time goes in v2:
time: 286 us; the launch traced here: 281 us
  waiting for transfers between devices  99.9 us (35%)
  starting transfers between devices  50.4 us (18%)
  matrix products  46.6 us (16%)
  other arithmetic  37.1 us (13%)
  local copies, waits for them, and re-layouts  25.2 us (9%)
  Pallas kernels  19.8 us (7%)
    ppermute x24, waiting for transfers between devices, along(): return lax.ppermute(value, 'dp', [(i, i ^ 1 << bit) for i in range(size)])  65.7 us
    dot_general x18, matrix products, dot32(): lax.dot_general(left, right, dims, preferred_element_type=jnp.float32)  46.6 us
    ppermute x24, starting transfers between devices, along(): return lax.ppermute(value, 'dp', [(i, i ^ 1 << bit) for i in range(size)])  33.2 us
    ppermute x9, waiting for transfers between devices, from_far(): return lax.ppermute(value, 'tensor', far)  18.5 us
    ppermute x4, waiting for transfers between devices, from_beside(): return lax.ppermute(value, 'dp', beside)  13.5 us
    pallas_call x1, Pallas kernels, attend_backward(): pl.pallas_call(attend_backward_kernel, grid_spec=pltpu.PrefetchScalarGrid...  11.6 us
    ppermute x9, starting transfers between devices, from_far(): return lax.ppermute(value, 'tensor', far)  11.1 us
    pallas_call x1, Pallas kernels, attend_forward(): pl.pallas_call(attend_forward_kernel, grid_spec=pltpu.PrefetchScalarGridS...  8.2 us
  transfers between devices with their start and end apart: 46, of which 19 were waited for; matrix products, arithmetic and copies ran while one was open for 31% of the time, Pallas kernels for 7%

profile of v2, /device:TPU:0, one launch (start us, length us, event | category | flops | bytes accessed | tf_op | source)
XLA Modules:
  0.0 281.0 jit_solution(3379770945697475480)
XLA Ops:
  2.2 3.0 %collective-permute-start.2 = (f32[1152]{0:T(1024)S(1)}, f32[1152]{0:T(1024)S(1)}, u32[]{:S(2)}, u32[]{:S(2)}) collective-permute-start(f32[1152]{0:T(1024)S(1)} %pad_maximum_fusion.27), channel_id=1, source_target_pairs={{0,2},{1,3},{2,0},{3,1},{4,6},{5,7},{6,4},{7,5},{8,10},{9,11},{10,... | collective-permute-start | bytes 13832 | tf_op jit(solution)/shard_map/ppermute | solution.py:272
  18.0 7.6 %collective-permute-done.7 = bf16[96,768]{1,0:T(8,128)(2,1)} collective-permute-done((bf16[96,768]{1,0:T(8,128)(2,1)S(1)}, bf16[96,768]{1,0:T(8,128)(2,1)}, u32[]{:S(2)}, u32[]{:S(2)}) %collective-permute-start.7) | collective-permute-done | bytes 147488 | tf_op jit(solution)/shard_map/ppermute | solution.py:272
  28.9 3.6 %collective-permute-done.8 = bf16[96,768]{1,0:T(8,128)(2,1)S(1)} collective-permute-done((bf16[96,768]{1,0:T(8,128)(2,1)}, bf16[96,768]{1,0:T(8,128)(2,1)S(1)}, u32[]{:S(2)}, u32[]{:S(2)}) %collective-permute-start.8) | collective-permute-done | bytes 147488 | tf_op jit(solution)/shard_map/ppermute | solution.py:280
  33.8 4.4 %collective-permute-done.1 = bf16[384,768]{1,0:T(8,128)(2,1)} collective-permute-done((bf16[384,768]{1,0:T(8,128)(2,1)S(1)}, bf16[384,768]{1,0:T(8,128)(2,1)}, u32[]{:S(2)}, u32[]{:S(2)}) %collective-permute-start.1) | collective-permute-done | bytes 589856 | tf_op jit(solution)/shard_map/ppermute | solution.py:272
  44.2 8.2 %attend_forward.1 = (bf16[1024,384]{1,0:T(8,128)(2,1)S(1)}, f32[3,8,1024]{2,1,0:T(8,128)S(1)}) custom-call(s32[1]{0:T(128)} %bitcast.core_ref, bf16[1024,1152]{1,0:T(8,128)(2,1)S(1)} %add_convert_fusion.qkv_ref), custom_call_target="tpu_custom_call" | custom-call | flops 2013265920 | bytes 3145728 | tf_op jit(solution)/shard_map/attend_forward/pallas_call | solution.py:170
  63.8 3.7 %convolution_add_fusion = f32[1024,1536]{1,0:T(8,128)S(1)} fusion(f32[1536]{0:T(1024)S(1)} %pad_maximum_fusion.28, bf16[768,768]{1,0:T(8,128)(2,1)S(1)} %maximum_select_fusion, bf16[768,768]{1,0:T(8,128)(2,1)S(1)} %copy-done.17, bf16[512,768]{1,0:T(8,128)(2,1)} %collective-permute-done.10, bf16[512,768]{1,0:T(8,128)(2,1)S(1)} %add_convert_fusion.4), kind=kOutput, calls=%fused_computation.13 | convolution fusion | flops 2425356288 | bytes 10229760 | tf_op jit(solution)/shard_map/dot_general | solution.py:38
  67.6 9.8 %collective-permute-done.11 = bf16[384,768]{1,0:T(8,128)(2,1)S(1)} collective-permute-done((bf16[384,768]{1,0:T(8,128)(2,1)}, bf16[384,768]{1,0:T(8,128)(2,1)S(1)}, u32[]{:S(2)}, u32[]{:S(2)}) %collective-permute-start.11) | collective-permute-done | bytes 589856 | tf_op jit(solution)/shard_map/ppermute | solution.py:280
  81.2 9.0 %convert_reduce_fusion = (f32[1536]{0:T(1024)S(1)}, bf16[1024,1536]{1,0:T(8,128)(2,1)S(1)}) fusion(f32[1024,1536]{1,0:T(8,128)S(1)} %convolution_add_fusion, bf16[1024,768]{1,0:T(8,128)(2,1)S(1)} %constant_dynamic-update-slice_fusion, bf16[768,768]{1,0:T(8,128)(2,1)S(1)} %maximum_select_fusion.1, bf16[768,768]{1,0:T(8,128)(2,1)S(1)} %copy-done.19), kind=kOutput, calls=%fused_computation.9 | convolution fusion | flops 2455239168 | bytes 13375488 | tf_op jit(solution)/shard_map/dot_general | solution.py:38
  93.0 2.5 fusion.42
  96.5 3.6 %fusion.39 = bf16[768,768]{1,0:T(8,128)(2,1)} fusion(bf16[1024,1536]{1,0:T(8,128)(2,1)S(1)} %get-tuple-element.73, bf16[512,768]{1,0:T(8,128)(2,1)} %collective-permute-done.10, bf16[512,768]{1,0:T(8,128)(2,1)S(1)} %add_convert_fusion.4), kind=kOutput, calls=%fused_computation.70 | convolution fusion | flops 1211695104 | bytes 4325376 | tf_op jit(solution)/shard_map/dot_general | solution.py:38
  101.6 2.9 %fusion.27 = f32[768,768]{1,0:T(8,128)} fusion(bf16[1024,768]{1,0:T(8,128)(2,1)S(1)} %constant_dynamic-update-slice_fusion, bf16[1024,1536]{1,0:T(8,128)(2,1)S(1)} %multiply_convert_fusion), kind=kOutput, calls=%fused_computation.47 | convolution fusion | flops 1207959552 | bytes 5505024 | tf_op jit(solution)/shard_map/dot_general | solution.py:38
  106.9 3.6 %convert_reduce_fusion.4 = (f32[768]{0:T(1024)}, bf16[512,768]{1,0:T(8,128)(2,1)S(1)}, f32[512,768]{1,0:T(8,128)}, f32[768]{0:T(1024)}) fusion(f32[512]{0:T(512)S(1)} %get-tuple-element.74, f32[512,768]{1,0:T(8,128)S(1)} %get-tuple-element.69, f32[512]{0:T(512)S(1)} %broadcast_multiply_fusion.4, f32[512]{0:T(512)S(1)} %get-tuple-element.75, ...), kind=kLoop, calls=%fused_computation.63 | loop fusion | flops 5110272 | bytes 6308864 | tf_op jit(solution)/shard_map/reduce_sum | solution.py:370
  110.5 4.0 %fusion.29 = f32[768,768]{1,0:T(8,128)} fusion(bf16[1024,1536]{1,0:T(8,128)(2,1)S(1)} %get-tuple-element.73, bf16[512,768]{1,0:T(8,128)(2,1)} %collective-permute-done.10, bf16[512,768]{1,0:T(8,128)(2,1)S(1)} %add_convert_fusion.4), kind=kOutput, calls=%fused_computation.49 | convolution fusion | flops 1211105280 | bytes 5505024 | tf_op jit(solution)/shard_map/dot_general | solution.py:38
  119.1 11.6 %attend_backward.1 = bf16[1024,1152]{1,0:T(8,128)(2,1)S(1)} custom-call(s32[1]{0:T(128)} %bitcast.core_ref, bf16[1024,1152]{1,0:T(8,128)(2,1)S(1)} %copy-done.1, bf16[1024,384]{1,0:T(8,128)(2,1)S(1)} %get-tuple-element.34.out_ref, f32[3,8,1024]{2,1,0:T(8,128)S(1)} %get-tuple-element.40.log_ref, bf16[1024,384]{1,0:T(8,128)(2,1)S(1)} %convolution_convert_fusion.grad_ref), custom_call_target="tpu_custom_call" | custom-call | flops 5637144576 | bytes 6291456 | tf_op jit(solution)/shard_map/attend_backward/pallas_call | solution.py:194
  138.1 2.4 add_convert_fusion.1
  143.0 6.5 %collective-permute-done.32 = bf16[768,768]{1,0:T(8,128)(2,1)} collective-permute-done((bf16[768,768]{1,0:T(8,128)(2,1)}, bf16[768,768]{1,0:T(8,128)(2,1)}, u32[]{:S(2)}, u32[]{:S(2)}) %collective-permute-start.32) | collective-permute-done | bytes 1179680 | tf_op jit(solution)/shard_map/ppermute | solution.py:272
  164.6 2.9 %collective-permute-start.41 = (bf16[192,768]{1,0:T(8,128)(2,1)S(1)}, bf16[192,768]{1,0:T(8,128)(2,1)S(1)}, u32[]{:S(2)}, u32[]{:S(2)}) collective-permute-start(bf16[192,768]{1,0:T(8,128)(2,1)S(1)} %constant_dynamic-slice_fusion.1), channel_id=1, source_target_pairs={{0,16},{4,20},{8,24},{12,28},{16,0},{20,4},{24,8},{28,12},{1,17},{... | collective-permute-start | bytes 884744 | tf_op jit(solution)/shard_map/ppermute | solution.py:222
  170.4 2.8 fusion.20
  176.8 2.9 %collective-permute-done.41 = bf16[192,768]{1,0:T(8,128)(2,1)S(1)} collective-permute-done((bf16[192,768]{1,0:T(8,128)(2,1)S(1)}, bf16[192,768]{1,0:T(8,128)(2,1)S(1)}, u32[]{:S(2)}, u32[]{:S(2)}) %collective-permute-start.41) | collective-permute-done | bytes 294944 | tf_op jit(solution)/shard_map/ppermute | solution.py:222
  186.7 5.2 %collective-permute-done.35 = bf16[96,768]{1,0:T(8,128)(2,1)S(1)} collective-permute-done((bf16[96,768]{1,0:T(8,128)(2,1)S(1)}, bf16[96,768]{1,0:T(8,128)(2,1)S(1)}, u32[]{:S(2)}, u32[]{:S(2)}) %collective-permute-start.35) | collective-permute-done | bytes 147488 | tf_op jit(solution)/shard_map/ppermute | solution.py:222
  192.1 3.0 %collective-permute-start.44 = (bf16[192,768]{1,0:T(8,128)(2,1)S(1)}, bf16[192,768]{1,0:T(8,128)(2,1)S(1)}, u32[]{:S(2)}, u32[]{:S(2)}) collective-permute-start(bf16[192,768]{1,0:T(8,128)(2,1)S(1)} %maximum_select_fusion.13), channel_id=1, source_target_pairs={{0,16},{4,20},{8,24},{12,28},{16,0},{20,4},{24,8},{28,12},{1,17},{... | collective-permute-start | bytes 884744 | tf_op jit(solution)/shard_map/ppermute | solution.py:222
  195.1 11.4 %collective-permute-done.36 = bf16[96,768]{1,0:T(8,128)(2,1)S(1)} collective-permute-done((bf16[96,768]{1,0:T(8,128)(2,1)S(1)}, bf16[96,768]{1,0:T(8,128)(2,1)S(1)}, u32[]{:S(2)}, u32[]{:S(2)}) %collective-permute-start.36) | collective-permute-done | bytes 147488 | tf_op jit(solution)/shard_map/ppermute | solution.py:222
  212.4 4.1 %collective-permute-done.37 = bf16[192,768]{1,0:T(8,128)(2,1)S(1)} collective-permute-done((bf16[192,768]{1,0:T(8,128)(2,1)S(1)}, bf16[192,768]{1,0:T(8,128)(2,1)S(1)}, u32[]{:S(2)}, u32[]{:S(2)}) %collective-permute-start.37) | collective-permute-done | bytes 294944 | tf_op jit(solution)/shard_map/ppermute | solution.py:222
  218.2 4.6 %collective-permute-done.20 = bf16[192,768]{1,0:T(8,128)(2,1)S(1)} collective-permute-done((bf16[192,768]{1,0:T(8,128)(2,1)S(1)}, bf16[192,768]{1,0:T(8,128)(2,1)S(1)}, u32[]{:S(2)}, u32[]{:S(2)}) %collective-permute-start.20) | collective-permute-done | bytes 294944 | tf_op jit(solution)/shard_map/ppermute | solution.py:222
  224.1 8.4 %collective-permute-done.21 = bf16[96,768]{1,0:T(8,128)(2,1)S(1)} collective-permute-done((bf16[96,768]{1,0:T(8,128)(2,1)S(1)}, bf16[96,768]{1,0:T(8,128)(2,1)S(1)}, u32[]{:S(2)}, u32[]{:S(2)}) %collective-permute-start.21) | collective-permute-done | bytes 147488 | tf_op jit(solution)/shard_map/ppermute | solution.py:222
  234.2 4.5 %collective-permute-start.27 = (bf16[128,768]{1,0:T(8,128)(2,1)S(1)}, bf16[128,768]{1,0:T(8,128)(2,1)S(1)}, u32[]{:S(2)}, u32[]{:S(2)}) collective-permute-start(bf16[128,768]{1,0:T(8,128)(2,1)S(1)} %constant_dynamic-slice_fusion.7), channel_id=1, source_target_pairs={{0,8},{4,12},{8,0},{12,4},{16,24},{20,28},{24,16},{28,20},{1,9},{5... | collective-permute-start | bytes 589832 | tf_op jit(solution)/shard_map/ppermute | solution.py:222
  239.0 3.3 %collective-permute-done.27 = bf16[128,768]{1,0:T(8,128)(2,1)S(1)} collective-permute-done((bf16[128,768]{1,0:T(8,128)(2,1)S(1)}, bf16[128,768]{1,0:T(8,128)(2,1)S(1)}, u32[]{:S(2)}, u32[]{:S(2)}) %collective-permute-start.27) | collective-permute-done | bytes 196640 | tf_op jit(solution)/shard_map/ppermute | solution.py:222
  245.5 8.5 %collective-permute-done.28 = bf16[64,768]{1,0:T(8,128)(2,1)S(1)} collective-permute-done((bf16[64,768]{1,0:T(8,128)(2,1)S(1)}, bf16[64,768]{1,0:T(8,128)(2,1)S(1)}, u32[]{:S(2)}, u32[]{:S(2)}) %collective-permute-start.28) | collective-permute-done | bytes 98336 | tf_op jit(solution)/shard_map/ppermute | solution.py:222
  254.1 3.1 %collective-permute-done.24 = bf16[96,768]{1,0:T(8,128)(2,1)S(1)} collective-permute-done((bf16[96,768]{1,0:T(8,128)(2,1)S(1)}, bf16[96,768]{1,0:T(8,128)(2,1)S(1)}, u32[]{:S(2)}, u32[]{:S(2)}) %collective-permute-start.24) | collective-permute-done | bytes 147488 | tf_op jit(solution)/shard_map/ppermute | solution.py:222
  258.3 2.7 collective-permute-done.29
  264.3 5.3 %collective-permute-done.30 = bf16[128,768]{1,0:T(8,128)(2,1)S(1)} collective-permute-done((bf16[128,768]{1,0:T(8,128)(2,1)S(1)}, bf16[128,768]{1,0:T(8,128)(2,1)S(1)}, u32[]{:S(2)}, u32[]{:S(2)}) %collective-permute-start.30) | collective-permute-done | bytes 196640 | tf_op jit(solution)/shard_map/ppermute | solution.py:222
  274.5 4.6 %collective-permute-done.31 = bf16[256,768]{1,0:T(8,128)(2,1)S(1)} collective-permute-done((bf16[256,768]{1,0:T(8,128)(2,1)S(1)}, bf16[256,768]{1,0:T(8,128)(2,1)S(1)}, u32[]{:S(2)}, u32[]{:S(2)}) %collective-permute-start.31) | collective-permute-done | bytes 393248 | tf_op jit(solution)/shard_map/ppermute | solution.py:222
  (288 shorter events, 115.4 us)
Async XLA Ops:
  9.1 17.9 %collective-permute-start.3 = (bf16[3,384,192]{1,2,0:T(8,128)(2,1)S(1)}, bf16[3,384,192]{1,2,0:T(8,128)(2,1)}, u32[]{:S(2)}, u32[]{:S(2)}) collective-permute-start(bf16[3,384,192]{1,2,0:T(8,128)(2,1)S(1)} %constant_dynamic-slice_fusion.14), channel_id=1, source_target_pairs={{0,2},{1,3},{2,0},{3,1},{4,6},{5,7},{6,4},{7,5},{8,10},{9,11},{10,... | collective-permute-start | bytes 1327112 | tf_op jit(solution)/shard_map/ppermute | solution.py:272
  9.6 24.0 %collective-permute-start = (bf16[512,768]{1,0:T(8,128)(2,1)S(1)}, bf16[512,768]{1,0:T(8,128)(2,1)S(1)}, u32[]{:S(2)}, u32[]{:S(2)}) collective-permute-start(bf16[512,768]{1,0:T(8,128)(2,1)S(1)} %fusion.15), channel_id=1, source_target_pairs={{0,1},{1,0},{2,3},{3,2},{4,5},{5,4},{6,7},{7,6},{8,9},{9,8},{10,11... | collective-permute-start | bytes 2359304 | tf_op jit(solution)/shard_map/ppermute | solution.py:269
  9.8 15.8 %collective-permute-start.7 = (bf16[96,768]{1,0:T(8,128)(2,1)S(1)}, bf16[96,768]{1,0:T(8,128)(2,1)}, u32[]{:S(2)}, u32[]{:S(2)}) collective-permute-start(bf16[96,768]{1,0:T(8,128)(2,1)S(1)} %constant_dynamic-slice_fusion.12), channel_id=1, source_target_pairs={{0,2},{1,3},{2,0},{3,1},{4,6},{5,7},{6,4},{7,5},{8,10},{9,11},{10,... | collective-permute-start | bytes 442376 | tf_op jit(solution)/shard_map/ppermute | solution.py:272
  12.9 25.3 %collective-permute-start.1 = (bf16[384,768]{1,0:T(8,128)(2,1)S(1)}, bf16[384,768]{1,0:T(8,128)(2,1)}, u32[]{:S(2)}, u32[]{:S(2)}) collective-permute-start(bf16[384,768]{1,0:T(8,128)(2,1)S(1)} %constant_dynamic-slice_fusion.15), channel_id=1, source_target_pairs={{0,2},{1,3},{2,0},{3,1},{4,6},{5,7},{6,4},{7,5},{8,10},{9,11},{10,... | collective-permute-start | bytes 1769480 | tf_op jit(solution)/shard_map/ppermute | solution.py:272
  14.0 38.5 %collective-permute-start.6 = (bf16[384,768]{1,0:T(8,128)(2,1)}, bf16[384,768]{1,0:T(8,128)(2,1)}, u32[]{:S(2)}, u32[]{:S(2)}) collective-permute-start(bf16[384,768]{1,0:T(8,128)(2,1)} %constant_dynamic-slice_fusion.13), channel_id=1, source_target_pairs={{0,2},{1,3},{2,0},{3,1},{4,6},{5,7},{6,4},{7,5},{8,10},{9,11},{10,... | collective-permute-start | bytes 1769480 | tf_op jit(solution)/shard_map/ppermute | solution.py:272
  27.1 12.6 %collective-permute-start.4 = (bf16[3,384,192]{1,2,0:T(8,128)(2,1)}, bf16[3,384,192]{1,2,0:T(8,128)(2,1)S(1)}, u32[]{:S(2)}, u32[]{:S(2)}) collective-permute-start(bf16[3,384,192]{1,2,0:T(8,128)(2,1)} %collective-permute-done.3), channel_id=1, source_target_pairs={{0,4},{4,0},{8,12},{12,8},{16,20},{20,16},{24,28},{28,24},{1,5},{5... | collective-permute-start | bytes 1327112 | tf_op jit(solution)/shard_map/ppermute | solution.py:280
  38.2 14.2 %collective-permute-start.5 = (bf16[384,768]{1,0:T(8,128)(2,1)}, bf16[384,768]{1,0:T(8,128)(2,1)S(1)}, u32[]{:S(2)}, u32[]{:S(2)}) collective-permute-start(bf16[384,768]{1,0:T(8,128)(2,1)} %collective-permute-done.1), channel_id=1, source_target_pairs={{0,4},{4,0},{8,12},{12,8},{16,20},{20,16},{24,28},{28,24},{1,5},{5... | collective-permute-start | bytes 1769480 | tf_op jit(solution)/shard_map/ppermute | solution.py:280
  61.6 15.9 %collective-permute-start.11 = (bf16[384,768]{1,0:T(8,128)(2,1)}, bf16[384,768]{1,0:T(8,128)(2,1)S(1)}, u32[]{:S(2)}, u32[]{:S(2)}) collective-permute-start(bf16[384,768]{1,0:T(8,128)(2,1)} %collective-permute-done.6), channel_id=1, source_target_pairs={{0,4},{4,0},{8,12},{12,8},{16,20},{20,16},{24,28},{28,24},{1,5},{5... | collective-permute-start | bytes 1769480 | tf_op jit(solution)/shard_map/ppermute | solution.py:280
  93.0 11.6 %collective-permute-start.14 = (bf16[512,768]{1,0:T(8,128)(2,1)S(1)}, bf16[512,768]{1,0:T(8,128)(2,1)S(1)}, u32[]{:S(2)}, u32[]{:S(2)}) collective-permute-start(bf16[512,768]{1,0:T(8,128)(2,1)S(1)} %fusion.52), channel_id=1, source_target_pairs={{0,1},{1,0},{2,3},{3,2},{4,5},{5,4},{6,7},{7,6},{8,9},{9,8},{10,11... | collective-permute-start | bytes 2359304 | tf_op jit(solution)/shard_map/ppermute | solution.py:269
  95.5 19.6 %collective-permute-start.12 = (bf16[512,768]{1,0:T(8,128)(2,1)S(1)}, bf16[512,768]{1,0:T(8,128)(2,1)S(1)}, u32[]{:S(2)}, u32[]{:S(2)}) collective-permute-start(bf16[512,768]{1,0:T(8,128)(2,1)S(1)} %fusion.49), channel_id=1, source_target_pairs={{0,1},{1,0},{2,3},{3,2},{4,5},{5,4},{6,7},{7,6},{8,9},{9,8},{10,11... | collective-permute-start | bytes 2359304 | tf_op jit(solution)/shard_map/ppermute | solution.py:269
  96.0 42.1 %collective-permute-start.39 = (bf16[768,768]{1,0:T(8,128)(2,1)}, bf16[768,768]{1,0:T(8,128)(2,1)}, u32[]{:S(2)}, u32[]{:S(2)}) collective-permute-start(bf16[768,768]{1,0:T(8,128)(2,1)} %fusion.42), channel_id=1, source_target_pairs={{0,2},{1,3},{2,0},{3,1},{4,6},{5,7},{6,4},{7,5},{8,10},{9,11},{10,... | collective-permute-start | bytes 3538952 | tf_op jit(solution)/shard_map/ppermute | solution.py:272
  100.1 49.4 %collective-permute-start.32 = (bf16[768,768]{1,0:T(8,128)(2,1)}, bf16[768,768]{1,0:T(8,128)(2,1)}, u32[]{:S(2)}, u32[]{:S(2)}) collective-permute-start(bf16[768,768]{1,0:T(8,128)(2,1)} %fusion.39), channel_id=1, source_target_pairs={{0,2},{1,3},{2,0},{3,1},{4,6},{5,7},{6,4},{7,5},{8,10},{9,11},{10,... | collective-permute-start | bytes 3538952 | tf_op jit(solution)/shard_map/ppermute | solution.py:272
  136.5 34.0 %collective-permute-start.16 = (bf16[512,768]{1,0:T(8,128)(2,1)}, bf16[512,768]{1,0:T(8,128)(2,1)}, u32[]{:S(2)}, u32[]{:S(2)}) collective-permute-start(bf16[512,768]{1,0:T(8,128)(2,1)} %convolution_convert_fusion.1), channel_id=1, source_target_pairs={{0,1},{1,0},{2,3},{3,2},{4,5},{5,4},{6,7},{7,6},{8,9},{9,8},{10,11... | collective-permute-start | bytes 2359304 | tf_op jit(solution)/shard_map/ppermute | solution.py:269
  141.4 21.7 %collective-permute-start.40 = (bf16[384,768]{1,0:T(8,128)(2,1)}, bf16[384,768]{1,0:T(8,128)(2,1)}, u32[]{:S(2)}, u32[]{:S(2)}) collective-permute-start(bf16[384,768]{1,0:T(8,128)(2,1)} %constant_dynamic-slice_fusion.2), channel_id=1, source_target_pairs={{0,8},{4,12},{8,0},{12,4},{16,24},{20,28},{24,16},{28,20},{1,9},{5... | collective-permute-start | bytes 1769480 | tf_op jit(solution)/shard_map/ppermute | solution.py:222
  152.0 15.4 %collective-permute-start.33 = (bf16[384,768]{1,0:T(8,128)(2,1)}, bf16[384,768]{1,0:T(8,128)(2,1)}, u32[]{:S(2)}, u32[]{:S(2)}) collective-permute-start(bf16[384,768]{1,0:T(8,128)(2,1)} %constant_dynamic-slice_fusion.5), channel_id=1, source_target_pairs={{0,4},{4,0},{8,12},{12,8},{16,20},{20,16},{24,28},{28,24},{1,5},{5... | collective-permute-start | bytes 1769480 | tf_op jit(solution)/shard_map/ppermute | solution.py:222
  162.8 43.7 %collective-permute-start.17 = (bf16[768,768]{1,0:T(8,128)(2,1)}, bf16[768,768]{1,0:T(8,128)(2,1)}, u32[]{:S(2)}, u32[]{:S(2)}) collective-permute-start(bf16[768,768]{1,0:T(8,128)(2,1)} %pad_maximum_fusion.6), channel_id=1, source_target_pairs={{0,2},{1,3},{2,0},{3,1},{4,6},{5,7},{6,4},{7,5},{8,10},{9,11},{10,... | collective-permute-start | bytes 3538952 | tf_op jit(solution)/shard_map/ppermute | solution.py:272
  164.6 15.1 %collective-permute-start.41 = (bf16[192,768]{1,0:T(8,128)(2,1)S(1)}, bf16[192,768]{1,0:T(8,128)(2,1)S(1)}, u32[]{:S(2)}, u32[]{:S(2)}) collective-permute-start(bf16[192,768]{1,0:T(8,128)(2,1)S(1)} %constant_dynamic-slice_fusion.1), channel_id=1, source_target_pairs={{0,16},{4,20},{8,24},{12,28},{16,0},{20,4},{24,8},{28,12},{1,17},{... | collective-permute-start | bytes 884744 | tf_op jit(solution)/shard_map/ppermute | solution.py:222
  168.8 12.6 %collective-permute-start.34 = (bf16[192,768]{1,0:T(8,128)(2,1)S(1)}, bf16[192,768]{1,0:T(8,128)(2,1)S(1)}, u32[]{:S(2)}, u32[]{:S(2)}) collective-permute-start(bf16[192,768]{1,0:T(8,128)(2,1)S(1)} %constant_dynamic-slice_fusion.4), channel_id=1, source_target_pairs={{0,8},{4,12},{8,0},{12,4},{16,24},{20,28},{24,16},{28,20},{1,9},{5... | collective-permute-start | bytes 884744 | tf_op jit(solution)/shard_map/ppermute | solution.py:222
  175.2 16.7 %collective-permute-start.19 = (f32[5760]{0:T(1024)S(1)}, f32[5760]{0:T(1024)S(1)}, u32[]{:S(2)}, u32[]{:S(2)}) collective-permute-start(f32[5760]{0:T(1024)S(1)} %fusion.71), channel_id=1, source_target_pairs={{0,2},{1,3},{2,0},{3,1},{4,6},{5,7},{6,4},{7,5},{8,10},{9,11},{10,... | collective-permute-start | bytes 69128 | tf_op jit(solution)/shard_map/ppermute | solution.py:272
  181.5 10.3 %collective-permute-start.35 = (bf16[96,768]{1,0:T(8,128)(2,1)S(1)}, bf16[96,768]{1,0:T(8,128)(2,1)S(1)}, u32[]{:S(2)}, u32[]{:S(2)}) collective-permute-start(bf16[96,768]{1,0:T(8,128)(2,1)S(1)} %constant_dynamic-slice_fusion.3), channel_id=1, source_target_pairs={{0,16},{4,20},{8,24},{12,28},{16,0},{20,4},{24,8},{28,12},{1,17},{... | collective-permute-start | bytes 442376 | tf_op jit(solution)/shard_map/ppermute | solution.py:222
  191.9 14.6 %collective-permute-start.36 = (bf16[96,768]{1,0:T(8,128)(2,1)S(1)}, bf16[96,768]{1,0:T(8,128)(2,1)S(1)}, u32[]{:S(2)}, u32[]{:S(2)}) collective-permute-start(bf16[96,768]{1,0:T(8,128)(2,1)S(1)} %add_convert_fusion.13), channel_id=1, source_target_pairs={{0,16},{4,20},{8,24},{12,28},{16,0},{20,4},{24,8},{28,12},{1,17},{... | collective-permute-start | bytes 442376 | tf_op jit(solution)/shard_map/ppermute | solution.py:222
  192.1 20.0 %collective-permute-start.44 = (bf16[192,768]{1,0:T(8,128)(2,1)S(1)}, bf16[192,768]{1,0:T(8,128)(2,1)S(1)}, u32[]{:S(2)}, u32[]{:S(2)}) collective-permute-start(bf16[192,768]{1,0:T(8,128)(2,1)S(1)} %maximum_select_fusion.13), channel_id=1, source_target_pairs={{0,16},{4,20},{8,24},{12,28},{16,0},{20,4},{24,8},{28,12},{1,17},{... | collective-permute-start | bytes 884744 | tf_op jit(solution)/shard_map/ppermute | solution.py:222
  206.5 10.0 %collective-permute-start.37 = (bf16[192,768]{1,0:T(8,128)(2,1)S(1)}, bf16[192,768]{1,0:T(8,128)(2,1)S(1)}, u32[]{:S(2)}, u32[]{:S(2)}) collective-permute-start(bf16[192,768]{1,0:T(8,128)(2,1)S(1)} %maximum_select_fusion.12), channel_id=1, source_target_pairs={{0,8},{4,12},{8,0},{12,4},{16,24},{20,28},{24,16},{28,20},{1,9},{5... | collective-permute-start | bytes 884744 | tf_op jit(solution)/shard_map/ppermute | solution.py:222
  208.5 14.3 %collective-permute-start.20 = (bf16[192,768]{1,0:T(8,128)(2,1)S(1)}, bf16[192,768]{1,0:T(8,128)(2,1)S(1)}, u32[]{:S(2)}, u32[]{:S(2)}) collective-permute-start(bf16[192,768]{1,0:T(8,128)(2,1)S(1)} %constant_dynamic-slice_fusion.11), channel_id=1, source_target_pairs={{0,8},{4,12},{8,0},{12,4},{16,24},{20,28},{24,16},{28,20},{1,9},{5... | collective-permute-start | bytes 884744 | tf_op jit(solution)/shard_map/ppermute | solution.py:222
  210.6 13.4 %collective-permute-start.26 = (bf16[256,768]{1,0:T(8,128)(2,1)S(1)}, bf16[256,768]{1,0:T(8,128)(2,1)S(1)}, u32[]{:S(2)}, u32[]{:S(2)}) collective-permute-start(bf16[256,768]{1,0:T(8,128)(2,1)S(1)} %constant_dynamic-slice_fusion.8), channel_id=1, source_target_pairs={{0,4},{4,0},{8,12},{12,8},{16,20},{20,16},{24,28},{28,24},{1,5},{5... | collective-permute-start | bytes 1179656 | tf_op jit(solution)/shard_map/ppermute | solution.py:222
  212.3 48.8 %collective-permute-start.45 = (bf16[384,768]{1,0:T(8,128)(2,1)S(1)}, bf16[384,768]{1,0:T(8,128)(2,1)S(1)}, u32[]{:S(2)}, u32[]{:S(2)}) collective-permute-start(bf16[384,768]{1,0:T(8,128)(2,1)S(1)} %maximum_select_fusion.8), channel_id=1, source_target_pairs={{0,8},{4,12},{8,0},{12,4},{16,24},{20,28},{24,16},{28,20},{1,9},{5... | collective-permute-start | bytes 1769480 | tf_op jit(solution)/shard_map/ppermute | solution.py:222
  216.7 46.0 %collective-permute-start.38 = (bf16[384,768]{1,0:T(8,128)(2,1)S(1)}, bf16[384,768]{1,0:T(8,128)(2,1)S(1)}, u32[]{:S(2)}, u32[]{:S(2)}) collective-permute-start(bf16[384,768]{1,0:T(8,128)(2,1)S(1)} %maximum_select_fusion.7), channel_id=1, source_target_pairs={{0,4},{4,0},{8,12},{12,8},{16,20},{20,16},{24,28},{28,24},{1,5},{5... | collective-permute-start | bytes 1769480 | tf_op jit(solution)/shard_map/ppermute | solution.py:222
  222.9 9.6 %collective-permute-start.21 = (bf16[96,768]{1,0:T(8,128)(2,1)S(1)}, bf16[96,768]{1,0:T(8,128)(2,1)S(1)}, u32[]{:S(2)}, u32[]{:S(2)}) collective-permute-start(bf16[96,768]{1,0:T(8,128)(2,1)S(1)} %constant_dynamic-slice_fusion.10), channel_id=1, source_target_pairs={{0,16},{4,20},{8,24},{12,28},{16,0},{20,4},{24,8},{28,12},{1,17},{... | collective-permute-start | bytes 442376 | tf_op jit(solution)/shard_map/ppermute | solution.py:222
  242.4 11.6 %collective-permute-start.28 = (bf16[64,768]{1,0:T(8,128)(2,1)S(1)}, bf16[64,768]{1,0:T(8,128)(2,1)S(1)}, u32[]{:S(2)}, u32[]{:S(2)}) collective-permute-start(bf16[64,768]{1,0:T(8,128)(2,1)S(1)} %constant_dynamic-slice_fusion.6), channel_id=1, source_target_pairs={{0,16},{4,20},{8,24},{12,28},{16,0},{20,4},{24,8},{28,12},{1,17},{... | collective-permute-start | bytes 294920 | tf_op jit(solution)/shard_map/ppermute | solution.py:222
  243.9 13.3 %collective-permute-start.24 = (bf16[96,768]{1,0:T(8,128)(2,1)S(1)}, bf16[96,768]{1,0:T(8,128)(2,1)S(1)}, u32[]{:S(2)}, u32[]{:S(2)}) collective-permute-start(bf16[96,768]{1,0:T(8,128)(2,1)S(1)} %maximum_select_fusion.15), channel_id=1, source_target_pairs={{0,16},{4,20},{8,24},{12,28},{16,0},{20,4},{24,8},{28,12},{1,17},{... | collective-permute-start | bytes 442376 | tf_op jit(solution)/shard_map/ppermute | solution.py:222
  257.2 14.1 %collective-permute-start.25 = (bf16[192,768]{1,0:T(8,128)(2,1)S(1)}, bf16[192,768]{1,0:T(8,128)(2,1)S(1)}, u32[]{:S(2)}, u32[]{:S(2)}) collective-permute-start(bf16[192,768]{1,0:T(8,128)(2,1)S(1)} %maximum_select_fusion.11), channel_id=1, source_target_pairs={{0,8},{4,12},{8,0},{12,4},{16,24},{20,28},{24,16},{28,20},{1,9},{5... | collective-permute-start | bytes 884744 | tf_op jit(solution)/shard_map/ppermute | solution.py:222
  269.8 9.3 %collective-permute-start.31 = (bf16[256,768]{1,0:T(8,128)(2,1)S(1)}, bf16[256,768]{1,0:T(8,128)(2,1)S(1)}, u32[]{:S(2)}, u32[]{:S(2)}) collective-permute-start(bf16[256,768]{1,0:T(8,128)(2,1)S(1)} %maximum_select_fusion.9), channel_id=1, source_target_pairs={{0,4},{4,0},{8,12},{12,8},{16,20},{20,16},{24,28},{28,24},{1,5},{5... | collective-permute-start | bytes 1179656 | tf_op jit(solution)/shard_map/ppermute | solution.py:222
  (60 other events, 358.8 us)

commit v3 on v2

--- a/solution.py
+++ b/solution.py
@@ -214,21 +214,38 @@
     )(core, qkv, attended, logs, out_grad)
 
 
-def sum_over_dp(rows, bits):
+def halves(rows, upper):
+    extent = rows.shape[-2] // 2
+    axis = rows.ndim - 2
+    kept = lax.dynamic_slice_in_dim(rows, upper * extent, extent, axis)
+    sent = lax.dynamic_slice_in_dim(rows, (1 - upper) * extent, extent, axis)
+    return kept, sent
+
+
+def joined(own, other):
+    return (own.astype(jnp.float32) + other.astype(jnp.float32)).astype(jnp.bfloat16)
+
+
+def sum_over_dp(rows, bits, far=None):
     place = lax.axis_index("dp")
     size = lax.axis_size("dp")
 
     def along(value, bit):
         return lax.ppermute(value, "dp", [(i, i ^ (1 << bit)) for i in range(size)])
 
-    for bit in bits:
-        extent = rows.shape[0] // 2
+    for step, bit in enumerate(bits):
         upper = (place >> bit) & 1
-        kept = lax.dynamic_slice_in_dim(rows, upper * extent, extent, 0)
-        sent = lax.dynamic_slice_in_dim(rows, (1 - upper) * extent, extent, 0)
-        rows = (kept.astype(jnp.float32) + along(sent, bit).astype(jnp.float32)).astype(
-            jnp.bfloat16
-        )
+        if step == 0 and far is not None:
+            kept, sent = halves(far, upper)
+            far = joined(kept, along(sent, bit))
+            kept, sent = halves(rows, upper)
+            rows = joined(kept, along(sent, bit))
+            size_t = lax.axis_size("tensor")
+            across = [(i, (i + size_t // 2) % size_t) for i in range(size_t)]
+            rows = joined(rows, lax.ppermute(far, "tensor", across))
+        else:
+            kept, sent = halves(rows, upper)
+            rows = joined(kept, along(sent, bit))
     for bit in reversed(bits):
         other = along(rows, bit)
         rows = jnp.where(
@@ -349,17 +366,12 @@
 
     columns_columns = (((0,), (0,)), ((), ()))
 
-    def joined(own, other):
-        return (own + other.astype(jnp.float32)).astype(jnp.bfloat16)
-
     proj_far = from_far(
         dot32(active_low[:, hidden_width:], grad_full, columns_columns).astype(jnp.bfloat16)
     )
     proj_own = dot32(active_low[:, :hidden_width], grad_full, columns_columns)
-    fc_far = from_far(
-        dot32(second, hidden_low[:, hidden_width:], columns_columns).astype(jnp.bfloat16)
-    )
-    fc_own = dot32(second, hidden_low[:, :hidden_width], columns_columns)
+    fc_other = dot32(second, hidden_low[:, hidden_width:], columns_columns).astype(jnp.bfloat16)
+    fc_own = dot32(second, hidden_low[:, :hidden_width], columns_columns).astype(jnp.bfloat16)
     fc_sums = jnp.sum(hidden_low, axis=0, dtype=jnp.float32)
 
     resid_grad = grad_rows + norm_back(second_grad, normed2, scale2, ln2_gain)
@@ -374,7 +386,7 @@
     qkv_grad = attend_backward(core, qkv, attended, logs, heads_grad)
     fc_own, proj_own, late_grad = lax.optimization_barrier((fc_own, proj_own, qkv_grad))
     bits = range(lax.axis_size("dp").bit_length() - 1)
-    fc_weight_grad = sum_over_dp(joined(fc_own, fc_far), [*bits]).astype(jnp.float32)
+    fc_weight_grad = sum_over_dp(fc_own, [*bits], fc_other).astype(jnp.float32)
     proj_weight_grad = sum_over_dp(joined(proj_own, proj_far), [*bits][1:] + [0]).astype(
         jnp.float32
     )

time: 286 us -> 275 us (0.962)
  waiting for transfers between devices: 99.9 us -> 90.6 us
    ppermute x9 -> x8, waiting for transfers between devices: 18.5 us -> 12 us  [from_far(): return lax.ppermute(value, 'tensor', far)]
    ppermute x24 -> x25, starting transfers between devices: 33.2 us -> 36 us  [along(): return lax.ppermute(value, 'dp', [(i, i ^ 1 << bit) for i in range(size)])]
    ppermute x24 -> x25, waiting for transfers between devices: 65.7 us -> 62.9 us  [along(): return lax.ppermute(value, 'dp', [(i, i ^ 1 << bit) for i in range(size)])]
    ppermute x9 -> x8, starting transfers between devices: 11.1 us -> 8.97 us  [from_far(): return lax.ppermute(value, 'tensor', far)]
  transfers between devices with their start and end apart: 46 -> 47, of which waited for: 19 -> 22; matrix products, arithmetic and copies ran while one was open for 31% -> 30% of each run, Pallas kernels for 7% -> 7%
where the time goes in v3:
time: 275 us; the launch traced here: 270 us
  waiting for transfers between devices  90.6 us (33%)
  starting transfers between devices  51.1 us (19%)
  matrix products  45.2 us (16%)
  other arithmetic  36.6 us (13%)
  local copies, waits for them, and re-layouts  25.1 us (9%)
  Pallas kernels  19.8 us (7%)
    ppermute x25, waiting for transfers between devices, along(): return lax.ppermute(value, 'dp', [(i, i ^ 1 << bit) for i in range(size)])  62.9 us
    dot_general x18, matrix products, dot32(): lax.dot_general(left, right, dims, preferred_element_type=jnp.float32)  45.2 us
    ppermute x25, starting transfers between devices, along(): return lax.ppermute(value, 'dp', [(i, i ^ 1 << bit) for i in range(size)])  36 us
    ppermute x4, waiting for transfers between devices, from_beside(): return lax.ppermute(value, 'dp', beside)  13.5 us
    ppermute x8, waiting for transfers between devices, from_far(): return lax.ppermute(value, 'tensor', far)  12 us
    pallas_call x1, Pallas kernels, attend_backward(): pl.pallas_call(attend_backward_kernel, grid_spec=pltpu.PrefetchScalarGrid...  11.6 us
    ppermute x8, starting transfers between devices, from_far(): return lax.ppermute(value, 'tensor', far)  8.97 us
    convert_element_type x15, other arithmetic, joined(): (own.astype(jnp.float32) + other.astype(jnp.float32)).astype(jnp.bfloat16)  8.37 us
  transfers between devices with their start and end apart: 47, of which 22 were waited for; matrix products, arithmetic and copies ran while one was open for 30% of the time, Pallas kernels for 7%

profile of v3, /device:TPU:0, one launch (start us, length us, event | category | flops | bytes accessed | tf_op | source)
XLA Modules:
  0.0 270.4 jit_solution(12736443184272841089)
XLA Ops:
  2.2 3.0 %collective-permute-start.2 = (f32[1152]{0:T(1024)S(1)}, f32[1152]{0:T(1024)S(1)}, u32[]{:S(2)}, u32[]{:S(2)}) collective-permute-start(f32[1152]{0:T(1024)S(1)} %pad_maximum_fusion.27), channel_id=1, source_target_pairs={{0,2},{1,3},{2,0},{3,1},{4,6},{5,7},{6,4},{7,5},{8,10},{9,11},{10,... | collective-permute-start | bytes 13832 | tf_op jit(solution)/shard_map/ppermute | solution.py:289
  18.0 7.6 %collective-permute-done.7 = bf16[96,768]{1,0:T(8,128)(2,1)} collective-permute-done((bf16[96,768]{1,0:T(8,128)(2,1)S(1)}, bf16[96,768]{1,0:T(8,128)(2,1)}, u32[]{:S(2)}, u32[]{:S(2)}) %collective-permute-start.7) | collective-permute-done | bytes 147488 | tf_op jit(solution)/shard_map/ppermute | solution.py:289
  28.9 3.6 %collective-permute-done.8 = bf16[96,768]{1,0:T(8,128)(2,1)S(1)} collective-permute-done((bf16[96,768]{1,0:T(8,128)(2,1)}, bf16[96,768]{1,0:T(8,128)(2,1)S(1)}, u32[]{:S(2)}, u32[]{:S(2)}) %collective-permute-start.8) | collective-permute-done | bytes 147488 | tf_op jit(solution)/shard_map/ppermute | solution.py:297
  33.8 4.4 %collective-permute-done.1 = bf16[384,768]{1,0:T(8,128)(2,1)} collective-permute-done((bf16[384,768]{1,0:T(8,128)(2,1)S(1)}, bf16[384,768]{1,0:T(8,128)(2,1)}, u32[]{:S(2)}, u32[]{:S(2)}) %collective-permute-start.1) | collective-permute-done | bytes 589856 | tf_op jit(solution)/shard_map/ppermute | solution.py:289
  44.2 8.2 %attend_forward.1 = (bf16[1024,384]{1,0:T(8,128)(2,1)S(1)}, f32[3,8,1024]{2,1,0:T(8,128)S(1)}) custom-call(s32[1]{0:T(128)} %bitcast.core_ref, bf16[1024,1152]{1,0:T(8,128)(2,1)S(1)} %add_convert_fusion.qkv_ref), custom_call_target="tpu_custom_call" | custom-call | flops 2013265920 | bytes 3145728 | tf_op jit(solution)/shard_map/attend_forward/pallas_call | solution.py:170
  63.8 3.7 %convolution_add_fusion = f32[1024,1536]{1,0:T(8,128)S(1)} fusion(f32[1536]{0:T(1024)S(1)} %pad_maximum_fusion.28, bf16[768,768]{1,0:T(8,128)(2,1)S(1)} %maximum_select_fusion, bf16[768,768]{1,0:T(8,128)(2,1)S(1)} %copy-done.16, bf16[512,768]{1,0:T(8,128)(2,1)} %collective-permute-done.10, bf16[512,768]{1,0:T(8,128)(2,1)S(1)} %add_convert_fusion.3), kind=kOutput, calls=%fused_computation.13 | convolution fusion | flops 2425356288 | bytes 10229760 | tf_op jit(solution)/shard_map/dot_general | solution.py:38
  67.6 9.9 %collective-permute-done.11 = bf16[384,768]{1,0:T(8,128)(2,1)S(1)} collective-permute-done((bf16[384,768]{1,0:T(8,128)(2,1)}, bf16[384,768]{1,0:T(8,128)(2,1)S(1)}, u32[]{:S(2)}, u32[]{:S(2)}) %collective-permute-start.11) | collective-permute-done | bytes 589856 | tf_op jit(solution)/shard_map/ppermute | solution.py:297
  81.1 9.0 %convert_reduce_fusion = (f32[1536]{0:T(1024)S(1)}, bf16[1024,1536]{1,0:T(8,128)(2,1)S(1)}) fusion(f32[1024,1536]{1,0:T(8,128)S(1)} %convolution_add_fusion, bf16[1024,768]{1,0:T(8,128)(2,1)S(1)} %constant_dynamic-update-slice_fusion, bf16[768,768]{1,0:T(8,128)(2,1)S(1)} %maximum_select_fusion.1, bf16[768,768]{1,0:T(8,128)(2,1)S(1)} %copy-done.18), kind=kOutput, calls=%fused_computation.9 | convolution fusion | flops 2455239168 | bytes 13375488 | tf_op jit(solution)/shard_map/dot_general | solution.py:38
  91.5 2.5 fusion.45
  96.0 2.6 fusion.42
  99.5 3.6 %fusion.39 = bf16[768,768]{1,0:T(8,128)(2,1)} fusion(bf16[1024,1536]{1,0:T(8,128)(2,1)S(1)} %get-tuple-element.73, bf16[512,768]{1,0:T(8,128)(2,1)} %collective-permute-done.10, bf16[512,768]{1,0:T(8,128)(2,1)S(1)} %add_convert_fusion.3), kind=kOutput, calls=%fused_computation.69 | convolution fusion | flops 1211695104 | bytes 4325376 | tf_op jit(solution)/shard_map/dot_general | solution.py:38
  103.2 2.9 %fusion.27 = f32[768,768]{1,0:T(8,128)} fusion(bf16[1024,768]{1,0:T(8,128)(2,1)S(1)} %constant_dynamic-update-slice_fusion, bf16[1024,1536]{1,0:T(8,128)(2,1)S(1)} %multiply_convert_fusion), kind=kOutput, calls=%fused_computation.46 | convolution fusion | flops 1207959552 | bytes 5505024 | tf_op jit(solution)/shard_map/dot_general | solution.py:38
  106.0 2.3 multiply_reduce_fusion
  108.4 3.6 %convert_reduce_fusion.4 = (f32[768]{0:T(1024)}, bf16[512,768]{1,0:T(8,128)(2,1)S(1)}, f32[512,768]{1,0:T(8,128)}, f32[768]{0:T(1024)}) fusion(f32[512]{0:T(512)S(1)} %get-tuple-element.74, f32[512,768]{1,0:T(8,128)S(1)} %get-tuple-element.69, f32[512]{0:T(512)S(1)} %broadcast_multiply_fusion.4, f32[512]{0:T(512)S(1)} %get-tuple-element.75, ...), kind=kLoop, calls=%fused_computation.62 | loop fusion | flops 5110272 | bytes 6308864 | tf_op jit(solution)/shard_map/reduce_sum | solution.py:382
  123.3 11.6 %attend_backward.1 = bf16[1024,1152]{1,0:T(8,128)(2,1)S(1)} custom-call(s32[1]{0:T(128)} %bitcast.core_ref, bf16[1024,1152]{1,0:T(8,128)(2,1)S(1)} %copy-done.1, bf16[1024,384]{1,0:T(8,128)(2,1)S(1)} %get-tuple-element.34.out_ref, f32[3,8,1024]{2,1,0:T(8,128)S(1)} %get-tuple-element.40.log_ref, bf16[1024,384]{1,0:T(8,128)(2,1)S(1)} %convolution_convert_fusion.grad_ref), custom_call_target="tpu_custom_call" | custom-call | flops 5637144576 | bytes 6291456 | tf_op jit(solution)/shard_map/attend_backward/pallas_call | solution.py:194
  161.1 2.7 collective-permute-start.42
  163.8 2.8 %fusion.20 = (f32[768]{0:T(1024)S(1)}, f32[512]{0:T(512)S(1)}, f32[512]{0:T(512)S(1)}, f32[768]{0:T(1024)S(1)}, f32[512,768]{1,0:T(8,128)S(1)}) fusion(bf16[512,768]{1,0:T(8,128)(2,1)S(1)} %copy-done.3, f32[512]{0:T(512)S(1)} %add_rsqrt_fusion.1, f32[512]{0:T(512)S(1)} %broadcast_multiply_fusion.5, f32[768]{0:T(1024)S(1)} %copy-done.25, ...), kind=kOutput, calls=%fused_computation.39 | convolution fusion | flops 910685696 | bytes 6113280 | tf_op jit(solution)/shard_map/dot_general | solution.py:38
  171.3 9.9 %collective-permute-done.42 = bf16[192,768]{1,0:T(8,128)(2,1)S(1)} collective-permute-done((bf16[192,768]{1,0:T(8,128)(2,1)S(1)}, bf16[192,768]{1,0:T(8,128)(2,1)S(1)}, u32[]{:S(2)}, u32[]{:S(2)}) %collective-permute-start.42) | collective-permute-done | bytes 294944 | tf_op jit(solution)/shard_map/ppermute | solution.py:234
  182.9 4.4 %collective-permute-done.43 = bf16[96,768]{1,0:T(8,128)(2,1)S(1)} collective-permute-done((bf16[96,768]{1,0:T(8,128)(2,1)S(1)}, bf16[96,768]{1,0:T(8,128)(2,1)S(1)}, u32[]{:S(2)}, u32[]{:S(2)}) %collective-permute-start.43) | collective-permute-done | bytes 147488 | tf_op jit(solution)/shard_map/ppermute | solution.py:234
  199.1 6.4 %collective-permute-done.38 = bf16[192,768]{1,0:T(8,128)(2,1)S(1)} collective-permute-done((bf16[192,768]{1,0:T(8,128)(2,1)S(1)}, bf16[192,768]{1,0:T(8,128)(2,1)S(1)}, u32[]{:S(2)}, u32[]{:S(2)}) %collective-permute-start.38) | collective-permute-done | bytes 294944 | tf_op jit(solution)/shard_map/ppermute | solution.py:234
  205.6 2.7 collective-permute-start.39
  209.3 2.5 collective-permute-done.20
  211.9 3.7 %collective-permute-start.21 = (bf16[96,768]{1,0:T(8,128)(2,1)S(1)}, bf16[96,768]{1,0:T(8,128)(2,1)S(1)}, u32[]{:S(2)}, u32[]{:S(2)}) collective-permute-start(bf16[96,768]{1,0:T(8,128)(2,1)S(1)} %constant_dynamic-slice_fusion.11), channel_id=1, source_target_pairs={{0,16},{4,20},{8,24},{12,28},{16,0},{20,4},{24,8},{28,12},{1,17},{... | collective-permute-start | bytes 442376 | tf_op jit(solution)/shard_map/ppermute | solution.py:234
  215.6 8.1 %collective-permute-done.21 = bf16[96,768]{1,0:T(8,128)(2,1)S(1)} collective-permute-done((bf16[96,768]{1,0:T(8,128)(2,1)S(1)}, bf16[96,768]{1,0:T(8,128)(2,1)S(1)}, u32[]{:S(2)}, u32[]{:S(2)}) %collective-permute-start.21) | collective-permute-done | bytes 147488 | tf_op jit(solution)/shard_map/ppermute | solution.py:234
  223.8 3.1 %collective-permute-start.22 = (bf16[48,768]{1,0:T(8,128)(2,1)S(1)}, bf16[48,768]{1,0:T(8,128)(2,1)S(1)}, u32[]{:S(2)}, u32[]{:S(2)}) collective-permute-start(bf16[48,768]{1,0:T(8,128)(2,1)S(1)} %constant_dynamic-slice_fusion.10), channel_id=1, source_target_pairs={{0,4},{4,0},{8,12},{12,8},{16,20},{20,16},{24,28},{28,24},{1,5},{5... | collective-permute-start | bytes 221192 | tf_op jit(solution)/shard_map/ppermute | solution.py:234
  227.0 2.6 collective-permute-start.27
  233.3 3.1 %collective-permute-start.28 = (bf16[64,768]{1,0:T(8,128)(2,1)S(1)}, bf16[64,768]{1,0:T(8,128)(2,1)S(1)}, u32[]{:S(2)}, u32[]{:S(2)}) collective-permute-start(bf16[64,768]{1,0:T(8,128)(2,1)S(1)} %constant_dynamic-slice_fusion.7), channel_id=1, source_target_pairs={{0,16},{4,20},{8,24},{12,28},{16,0},{20,4},{24,8},{28,12},{1,17},{... | collective-permute-start | bytes 294920 | tf_op jit(solution)/shard_map/ppermute | solution.py:234
  237.7 6.3 %collective-permute-done.28 = bf16[64,768]{1,0:T(8,128)(2,1)S(1)} collective-permute-done((bf16[64,768]{1,0:T(8,128)(2,1)S(1)}, bf16[64,768]{1,0:T(8,128)(2,1)S(1)}, u32[]{:S(2)}, u32[]{:S(2)}) %collective-permute-start.28) | collective-permute-done | bytes 98336 | tf_op jit(solution)/shard_map/ppermute | solution.py:234
  244.1 3.0 %collective-permute-done.24 = bf16[96,768]{1,0:T(8,128)(2,1)S(1)} collective-permute-done((bf16[96,768]{1,0:T(8,128)(2,1)S(1)}, bf16[96,768]{1,0:T(8,128)(2,1)S(1)}, u32[]{:S(2)}, u32[]{:S(2)}) %collective-permute-start.24) | collective-permute-done | bytes 147488 | tf_op jit(solution)/shard_map/ppermute | solution.py:234
  247.2 2.9 %collective-permute-done.29 = bf16[64,768]{1,0:T(8,128)(2,1)S(1)} collective-permute-done((bf16[64,768]{1,0:T(8,128)(2,1)S(1)}, bf16[64,768]{1,0:T(8,128)(2,1)S(1)}, u32[]{:S(2)}, u32[]{:S(2)}) %collective-permute-start.29) | collective-permute-done | bytes 98336 | tf_op jit(solution)/shard_map/ppermute | solution.py:234
  253.5 5.8 %collective-permute-done.30 = bf16[128,768]{1,0:T(8,128)(2,1)S(1)} collective-permute-done((bf16[128,768]{1,0:T(8,128)(2,1)S(1)}, bf16[128,768]{1,0:T(8,128)(2,1)S(1)}, u32[]{:S(2)}, u32[]{:S(2)}) %collective-permute-start.30) | collective-permute-done | bytes 196640 | tf_op jit(solution)/shard_map/ppermute | solution.py:234
  262.6 5.9 %collective-permute-done.31 = bf16[256,768]{1,0:T(8,128)(2,1)S(1)} collective-permute-done((bf16[256,768]{1,0:T(8,128)(2,1)S(1)}, bf16[256,768]{1,0:T(8,128)(2,1)S(1)}, u32[]{:S(2)}, u32[]{:S(2)}) %collective-permute-start.31) | collective-permute-done | bytes 393248 | tf_op jit(solution)/shard_map/ppermute | solution.py:234
  (289 shorter events, 114.2 us)
Async XLA Ops:
  9.1 17.9 %collective-permute-start.3 = (bf16[3,384,192]{1,2,0:T(8,128)(2,1)S(1)}, bf16[3,384,192]{1,2,0:T(8,128)(2,1)}, u32[]{:S(2)}, u32[]{:S(2)}) collective-permute-start(bf16[3,384,192]{1,2,0:T(8,128)(2,1)S(1)} %constant_dynamic-slice_fusion.15), channel_id=1, source_target_pairs={{0,2},{1,3},{2,0},{3,1},{4,6},{5,7},{6,4},{7,5},{8,10},{9,11},{10,... | collective-permute-start | bytes 1327112 | tf_op jit(solution)/shard_map/ppermute | solution.py:289
  9.6 24.0 %collective-permute-start = (bf16[512,768]{1,0:T(8,128)(2,1)S(1)}, bf16[512,768]{1,0:T(8,128)(2,1)S(1)}, u32[]{:S(2)}, u32[]{:S(2)}) collective-permute-start(bf16[512,768]{1,0:T(8,128)(2,1)S(1)} %fusion.15), channel_id=1, source_target_pairs={{0,1},{1,0},{2,3},{3,2},{4,5},{5,4},{6,7},{7,6},{8,9},{9,8},{10,11... | collective-permute-start | bytes 2359304 | tf_op jit(solution)/shard_map/ppermute | solution.py:286
  9.8 15.8 %collective-permute-start.7 = (bf16[96,768]{1,0:T(8,128)(2,1)S(1)}, bf16[96,768]{1,0:T(8,128)(2,1)}, u32[]{:S(2)}, u32[]{:S(2)}) collective-permute-start(bf16[96,768]{1,0:T(8,128)(2,1)S(1)} %constant_dynamic-slice_fusion.13), channel_id=1, source_target_pairs={{0,2},{1,3},{2,0},{3,1},{4,6},{5,7},{6,4},{7,5},{8,10},{9,11},{10,... | collective-permute-start | bytes 442376 | tf_op jit(solution)/shard_map/ppermute | solution.py:289
  12.9 25.3 %collective-permute-start.1 = (bf16[384,768]{1,0:T(8,128)(2,1)S(1)}, bf16[384,768]{1,0:T(8,128)(2,1)}, u32[]{:S(2)}, u32[]{:S(2)}) collective-permute-start(bf16[384,768]{1,0:T(8,128)(2,1)S(1)} %constant_dynamic-slice_fusion.16), channel_id=1, source_target_pairs={{0,2},{1,3},{2,0},{3,1},{4,6},{5,7},{6,4},{7,5},{8,10},{9,11},{10,... | collective-permute-start | bytes 1769480 | tf_op jit(solution)/shard_map/ppermute | solution.py:289
  14.0 38.4 %collective-permute-start.6 = (bf16[384,768]{1,0:T(8,128)(2,1)}, bf16[384,768]{1,0:T(8,128)(2,1)}, u32[]{:S(2)}, u32[]{:S(2)}) collective-permute-start(bf16[384,768]{1,0:T(8,128)(2,1)} %constant_dynamic-slice_fusion.14), channel_id=1, source_target_pairs={{0,2},{1,3},{2,0},{3,1},{4,6},{5,7},{6,4},{7,5},{8,10},{9,11},{10,... | collective-permute-start | bytes 1769480 | tf_op jit(solution)/shard_map/ppermute | solution.py:289
  27.1 12.6 %collective-permute-start.4 = (bf16[3,384,192]{1,2,0:T(8,128)(2,1)}, bf16[3,384,192]{1,2,0:T(8,128)(2,1)S(1)}, u32[]{:S(2)}, u32[]{:S(2)}) collective-permute-start(bf16[3,384,192]{1,2,0:T(8,128)(2,1)} %collective-permute-done.3), channel_id=1, source_target_pairs={{0,4},{4,0},{8,12},{12,8},{16,20},{20,16},{24,28},{28,24},{1,5},{5... | collective-permute-start | bytes 1327112 | tf_op jit(solution)/shard_map/ppermute | solution.py:297
  38.2 14.2 %collective-permute-start.5 = (bf16[384,768]{1,0:T(8,128)(2,1)}, bf16[384,768]{1,0:T(8,128)(2,1)S(1)}, u32[]{:S(2)}, u32[]{:S(2)}) collective-permute-start(bf16[384,768]{1,0:T(8,128)(2,1)} %collective-permute-done.1), channel_id=1, source_target_pairs={{0,4},{4,0},{8,12},{12,8},{16,20},{20,16},{24,28},{28,24},{1,5},{5... | collective-permute-start | bytes 1769480 | tf_op jit(solution)/shard_map/ppermute | solution.py:297
  61.5 15.9 %collective-permute-start.11 = (bf16[384,768]{1,0:T(8,128)(2,1)}, bf16[384,768]{1,0:T(8,128)(2,1)S(1)}, u32[]{:S(2)}, u32[]{:S(2)}) collective-permute-start(bf16[384,768]{1,0:T(8,128)(2,1)} %collective-permute-done.6), channel_id=1, source_target_pairs={{0,4},{4,0},{8,12},{12,8},{16,20},{20,16},{24,28},{28,24},{1,5},{5... | collective-permute-start | bytes 1769480 | tf_op jit(solution)/shard_map/ppermute | solution.py:297
  95.4 20.2 %collective-permute-start.12 = (bf16[512,768]{1,0:T(8,128)(2,1)S(1)}, bf16[512,768]{1,0:T(8,128)(2,1)S(1)}, u32[]{:S(2)}, u32[]{:S(2)}) collective-permute-start(bf16[512,768]{1,0:T(8,128)(2,1)S(1)} %fusion.52), channel_id=1, source_target_pairs={{0,1},{1,0},{2,3},{3,2},{4,5},{5,4},{6,7},{7,6},{8,9},{9,8},{10,11... | collective-permute-start | bytes 2359304 | tf_op jit(solution)/shard_map/ppermute | solution.py:286
  95.5 10.5 %collective-permute-start.14 = (bf16[512,768]{1,0:T(8,128)(2,1)S(1)}, bf16[512,768]{1,0:T(8,128)(2,1)S(1)}, u32[]{:S(2)}, u32[]{:S(2)}) collective-permute-start(bf16[512,768]{1,0:T(8,128)(2,1)S(1)} %fusion.55), channel_id=1, source_target_pairs={{0,1},{1,0},{2,3},{3,2},{4,5},{5,4},{6,7},{7,6},{8,9},{9,8},{10,11... | collective-permute-start | bytes 2359304 | tf_op jit(solution)/shard_map/ppermute | solution.py:286
  98.7 15.4 %collective-permute-start.33 = (bf16[384,768]{1,0:T(8,128)(2,1)S(1)}, bf16[384,768]{1,0:T(8,128)(2,1)S(1)}, u32[]{:S(2)}, u32[]{:S(2)}) collective-permute-start(bf16[384,768]{1,0:T(8,128)(2,1)S(1)} %constant_dynamic-slice_fusion.5), channel_id=1, source_target_pairs={{0,4},{4,0},{8,12},{12,8},{16,20},{20,16},{24,28},{28,24},{1,5},{5... | collective-permute-start | bytes 1769480 | tf_op jit(solution)/shard_map/ppermute | solution.py:234
  99.3 41.9 %collective-permute-start.40 = (bf16[768,768]{1,0:T(8,128)(2,1)}, bf16[768,768]{1,0:T(8,128)(2,1)}, u32[]{:S(2)}, u32[]{:S(2)}) collective-permute-start(bf16[768,768]{1,0:T(8,128)(2,1)} %fusion.45), channel_id=1, source_target_pairs={{0,2},{1,3},{2,0},{3,1},{4,6},{5,7},{6,4},{7,5},{8,10},{9,11},{10,... | collective-permute-start | bytes 3538952 | tf_op jit(solution)/shard_map/ppermute | solution.py:289
  115.1 40.8 %collective-permute-start.34 = (bf16[384,768]{1,0:T(8,128)(2,1)}, bf16[384,768]{1,0:T(8,128)(2,1)}, u32[]{:S(2)}, u32[]{:S(2)}) collective-permute-start(bf16[384,768]{1,0:T(8,128)(2,1)} %add_convert_fusion.6), channel_id=1, source_target_pairs={{0,2},{1,3},{2,0},{3,1},{4,6},{5,7},{6,4},{7,5},{8,10},{9,11},{10,... | collective-permute-start | bytes 1769480 | tf_op jit(solution)/shard_map/ppermute | solution.py:245
  137.0 26.8 %collective-permute-start.16 = (bf16[512,768]{1,0:T(8,128)(2,1)}, bf16[512,768]{1,0:T(8,128)(2,1)}, u32[]{:S(2)}, u32[]{:S(2)}) collective-permute-start(bf16[512,768]{1,0:T(8,128)(2,1)} %convolution_convert_fusion.1), channel_id=1, source_target_pairs={{0,1},{1,0},{2,3},{3,2},{4,5},{5,4},{6,7},{7,6},{8,9},{9,8},{10,11... | collective-permute-start | bytes 2359304 | tf_op jit(solution)/shard_map/ppermute | solution.py:286
  139.6 16.3 %collective-permute-start.32 = (bf16[384,768]{1,0:T(8,128)(2,1)}, bf16[384,768]{1,0:T(8,128)(2,1)}, u32[]{:S(2)}, u32[]{:S(2)}) collective-permute-start(bf16[384,768]{1,0:T(8,128)(2,1)} %constant_dynamic-slice_fusion.6), channel_id=1, source_target_pairs={{0,4},{4,0},{8,12},{12,8},{16,20},{20,16},{24,28},{28,24},{1,5},{5... | collective-permute-start | bytes 1769480 | tf_op jit(solution)/shard_map/ppermute | solution.py:234
  144.2 15.6 %collective-permute-start.41 = (bf16[384,768]{1,0:T(8,128)(2,1)}, bf16[384,768]{1,0:T(8,128)(2,1)}, u32[]{:S(2)}, u32[]{:S(2)}) collective-permute-start(bf16[384,768]{1,0:T(8,128)(2,1)} %constant_dynamic-slice_fusion.2), channel_id=1, source_target_pairs={{0,8},{4,12},{8,0},{12,4},{16,24},{20,28},{24,16},{28,20},{1,9},{5... | collective-permute-start | bytes 1769480 | tf_op jit(solution)/shard_map/ppermute | solution.py:234
  155.4 39.6 %collective-permute-start.17 = (bf16[768,768]{1,0:T(8,128)(2,1)}, bf16[768,768]{1,0:T(8,128)(2,1)}, u32[]{:S(2)}, u32[]{:S(2)}) collective-permute-start(bf16[768,768]{1,0:T(8,128)(2,1)} %pad_maximum_fusion.6), channel_id=1, source_target_pairs={{0,2},{1,3},{2,0},{3,1},{4,6},{5,7},{6,4},{7,5},{8,10},{9,11},{10,... | collective-permute-start | bytes 3538952 | tf_op jit(solution)/shard_map/ppermute | solution.py:289
  157.6 13.4 %collective-permute-start.35 = (bf16[192,768]{1,0:T(8,128)(2,1)S(1)}, bf16[192,768]{1,0:T(8,128)(2,1)S(1)}, u32[]{:S(2)}, u32[]{:S(2)}) collective-permute-start(bf16[192,768]{1,0:T(8,128)(2,1)S(1)} %constant_dynamic-slice_fusion.4), channel_id=1, source_target_pairs={{0,8},{4,12},{8,0},{12,4},{16,24},{20,28},{24,16},{28,20},{1,9},{5... | collective-permute-start | bytes 884744 | tf_op jit(solution)/shard_map/ppermute | solution.py:234
  161.1 20.1 %collective-permute-start.42 = (bf16[192,768]{1,0:T(8,128)(2,1)S(1)}, bf16[192,768]{1,0:T(8,128)(2,1)S(1)}, u32[]{:S(2)}, u32[]{:S(2)}) collective-permute-start(bf16[192,768]{1,0:T(8,128)(2,1)S(1)} %constant_dynamic-slice_fusion.1), channel_id=1, source_target_pairs={{0,16},{4,20},{8,24},{12,28},{16,0},{20,4},{24,8},{28,12},{1,17},{... | collective-permute-start | bytes 884744 | tf_op jit(solution)/shard_map/ppermute | solution.py:234
  168.5 20.3 %collective-permute-start.19 = (f32[5760]{0:T(1024)S(1)}, f32[5760]{0:T(1024)S(1)}, u32[]{:S(2)}, u32[]{:S(2)}) collective-permute-start(f32[5760]{0:T(1024)S(1)} %fusion.74), channel_id=1, source_target_pairs={{0,2},{1,3},{2,0},{3,1},{4,6},{5,7},{6,4},{7,5},{8,10},{9,11},{10,... | collective-permute-start | bytes 69128 | tf_op jit(solution)/shard_map/ppermute | solution.py:289
  171.2 11.6 %collective-permute-start.36 = (bf16[96,768]{1,0:T(8,128)(2,1)S(1)}, bf16[96,768]{1,0:T(8,128)(2,1)S(1)}, u32[]{:S(2)}, u32[]{:S(2)}) collective-permute-start(bf16[96,768]{1,0:T(8,128)(2,1)S(1)} %constant_dynamic-slice_fusion.3), channel_id=1, source_target_pairs={{0,16},{4,20},{8,24},{12,28},{16,0},{20,4},{24,8},{28,12},{1,17},{... | collective-permute-start | bytes 442376 | tf_op jit(solution)/shard_map/ppermute | solution.py:234
  189.7 15.7 %collective-permute-start.38 = (bf16[192,768]{1,0:T(8,128)(2,1)S(1)}, bf16[192,768]{1,0:T(8,128)(2,1)S(1)}, u32[]{:S(2)}, u32[]{:S(2)}) collective-permute-start(bf16[192,768]{1,0:T(8,128)(2,1)S(1)} %maximum_select_fusion.12), channel_id=1, source_target_pairs={{0,8},{4,12},{8,0},{12,4},{16,24},{20,28},{24,16},{28,20},{1,9},{5... | collective-permute-start | bytes 884744 | tf_op jit(solution)/shard_map/ppermute | solution.py:234
  192.6 15.7 %collective-permute-start.45 = (bf16[192,768]{1,0:T(8,128)(2,1)S(1)}, bf16[192,768]{1,0:T(8,128)(2,1)S(1)}, u32[]{:S(2)}, u32[]{:S(2)}) collective-permute-start(bf16[192,768]{1,0:T(8,128)(2,1)S(1)} %maximum_select_fusion.13), channel_id=1, source_target_pairs={{0,16},{4,20},{8,24},{12,28},{16,0},{20,4},{24,8},{28,12},{1,17},{... | collective-permute-start | bytes 884744 | tf_op jit(solution)/shard_map/ppermute | solution.py:234
  196.8 15.0 %collective-permute-start.20 = (bf16[192,768]{1,0:T(8,128)(2,1)S(1)}, bf16[192,768]{1,0:T(8,128)(2,1)S(1)}, u32[]{:S(2)}, u32[]{:S(2)}) collective-permute-start(bf16[192,768]{1,0:T(8,128)(2,1)S(1)} %constant_dynamic-slice_fusion.12), channel_id=1, source_target_pairs={{0,8},{4,12},{8,0},{12,4},{16,24},{20,28},{24,16},{28,20},{1,9},{5... | collective-permute-start | bytes 884744 | tf_op jit(solution)/shard_map/ppermute | solution.py:234
  198.5 17.0 %collective-permute-start.26 = (bf16[256,768]{1,0:T(8,128)(2,1)S(1)}, bf16[256,768]{1,0:T(8,128)(2,1)S(1)}, u32[]{:S(2)}, u32[]{:S(2)}) collective-permute-start(bf16[256,768]{1,0:T(8,128)(2,1)S(1)} %constant_dynamic-slice_fusion.9), channel_id=1, source_target_pairs={{0,4},{4,0},{8,12},{12,8},{16,20},{20,16},{24,28},{28,24},{1,5},{5... | collective-permute-start | bytes 1179656 | tf_op jit(solution)/shard_map/ppermute | solution.py:234
  205.6 44.6 %collective-permute-start.39 = (bf16[384,768]{1,0:T(8,128)(2,1)S(1)}, bf16[384,768]{1,0:T(8,128)(2,1)S(1)}, u32[]{:S(2)}, u32[]{:S(2)}) collective-permute-start(bf16[384,768]{1,0:T(8,128)(2,1)S(1)} %maximum_select_fusion.7), channel_id=1, source_target_pairs={{0,4},{4,0},{8,12},{12,8},{16,20},{20,16},{24,28},{28,24},{1,5},{5... | collective-permute-start | bytes 1769480 | tf_op jit(solution)/shard_map/ppermute | solution.py:234
  208.5 43.4 %collective-permute-start.46 = (bf16[384,768]{1,0:T(8,128)(2,1)S(1)}, bf16[384,768]{1,0:T(8,128)(2,1)S(1)}, u32[]{:S(2)}, u32[]{:S(2)}) collective-permute-start(bf16[384,768]{1,0:T(8,128)(2,1)S(1)} %maximum_select_fusion.8), channel_id=1, source_target_pairs={{0,8},{4,12},{8,0},{12,4},{16,24},{20,28},{24,16},{28,20},{1,9},{5... | collective-permute-start | bytes 1769480 | tf_op jit(solution)/shard_map/ppermute | solution.py:234
  211.9 11.9 %collective-permute-start.21 = (bf16[96,768]{1,0:T(8,128)(2,1)S(1)}, bf16[96,768]{1,0:T(8,128)(2,1)S(1)}, u32[]{:S(2)}, u32[]{:S(2)}) collective-permute-start(bf16[96,768]{1,0:T(8,128)(2,1)S(1)} %constant_dynamic-slice_fusion.11), channel_id=1, source_target_pairs={{0,16},{4,20},{8,24},{12,28},{16,0},{20,4},{24,8},{28,12},{1,17},{... | collective-permute-start | bytes 442376 | tf_op jit(solution)/shard_map/ppermute | solution.py:234
  233.3 10.7 %collective-permute-start.28 = (bf16[64,768]{1,0:T(8,128)(2,1)S(1)}, bf16[64,768]{1,0:T(8,128)(2,1)S(1)}, u32[]{:S(2)}, u32[]{:S(2)}) collective-permute-start(bf16[64,768]{1,0:T(8,128)(2,1)S(1)} %constant_dynamic-slice_fusion.7), channel_id=1, source_target_pairs={{0,16},{4,20},{8,24},{12,28},{16,0},{20,4},{24,8},{28,12},{1,17},{... | collective-permute-start | bytes 294920 | tf_op jit(solution)/shard_map/ppermute | solution.py:234
  236.4 10.7 %collective-permute-start.24 = (bf16[96,768]{1,0:T(8,128)(2,1)S(1)}, bf16[96,768]{1,0:T(8,128)(2,1)S(1)}, u32[]{:S(2)}, u32[]{:S(2)}) collective-permute-start(bf16[96,768]{1,0:T(8,128)(2,1)S(1)} %maximum_select_fusion.15), channel_id=1, source_target_pairs={{0,16},{4,20},{8,24},{12,28},{16,0},{20,4},{24,8},{28,12},{1,17},{... | collective-permute-start | bytes 442376 | tf_op jit(solution)/shard_map/ppermute | solution.py:234
  247.1 12.3 %collective-permute-start.25 = (bf16[192,768]{1,0:T(8,128)(2,1)S(1)}, bf16[192,768]{1,0:T(8,128)(2,1)S(1)}, u32[]{:S(2)}, u32[]{:S(2)}) collective-permute-start(bf16[192,768]{1,0:T(8,128)(2,1)S(1)} %maximum_select_fusion.11), channel_id=1, source_target_pairs={{0,8},{4,12},{8,0},{12,4},{16,24},{20,28},{24,16},{28,20},{1,9},{5... | collective-permute-start | bytes 884744 | tf_op jit(solution)/shard_map/ppermute | solution.py:234
  250.2 9.1 %collective-permute-start.30 = (bf16[128,768]{1,0:T(8,128)(2,1)S(1)}, bf16[128,768]{1,0:T(8,128)(2,1)S(1)}, u32[]{:S(2)}, u32[]{:S(2)}) collective-permute-start(bf16[128,768]{1,0:T(8,128)(2,1)S(1)} %maximum_select_fusion.14), channel_id=1, source_target_pairs={{0,8},{4,12},{8,0},{12,4},{16,24},{20,28},{24,16},{28,20},{1,9},{5... | collective-permute-start | bytes 589832 | tf_op jit(solution)/shard_map/ppermute | solution.py:234
  (60 other events, 365.0 us)
